TPU v7x, 768 devices: a whole 4x8x12 slice. The times are simulated.
768 devices in a mesh: dp: 24 (over z, y_hi), shard: 32 (over y_lo, x, core).
Axes of the slice: x: 4, y: 8 (y_hi: 2, y_lo: 4; y = y_hi * 4 + y_lo), z: 12, core: 2. Of those that a mesh axis runs over, the one named last changes fastest.
Arguments:
- out_grad: bfloat16 [12288, 8192], P('dp', 'shard'), may hold values from -6 to 6
- hidden: bfloat16 [12288, 24, 1024], P('dp', None, 'shard'), may hold values from -0.078125 to 0.078125
- basis: bfloat16 [8192, 1024], P('shard'), may hold values from -0.0625 to 0.0625
- moment: float32 [24576, 1024], P(('dp', 'shard')), may hold values from -3 to 3
- second: float32 [24576, 1024], P(('dp', 'shard')), may hold values from 0.001 to 0.01
Outputs:
- update: bfloat16 [24576, 8192], P('dp', 'shard')
- moment_new: float32 [24576, 1024], P(('dp', 'shard'))
- second_new: float32 [24576, 1024], P(('dp', 'shard'))
All inputs are finite; a program needn't handle non-finite values.
Results may differ from a plain program's by a relative error of at most 0.0052.
Values may be sent and summed in bfloat16 or wider, within the bound.
No kernel may reach another device: no remote copies, remote signals or barrier semaphores. Data moves between devices by JAX's collectives and lax.ppermute only.
A program may use at most 64 MiB of HBM per device.

v0:
```python
import jax
import jax.numpy as jnp
from jax import lax
from jax.sharding import PartitionSpec as P

STEP = 20


def contract_rows(left, right):
    return lax.dot_general(
        left, right, (((0,), (0,)), ((), ())), preferred_element_type=jnp.float32
    )


def per_device(out_grad, hidden, basis, moment, second):
    tok_rows = out_grad.shape[0]
    partial_basis = jnp.dot(out_grad, basis, preferred_element_type=jnp.float32)
    projected = lax.psum(partial_basis, "shard").astype(jnp.bfloat16)
    flat_hidden = hidden.reshape(tok_rows, -1)
    lowrank = lax.psum_scatter(
        contract_rows(flat_hidden, projected), "dp", scatter_dimension=0, tiled=True
    )
    moment_new = 0.9 * moment + 0.1 * lowrank
    second_new = 0.999 * second + 0.001 * lowrank * lowrank
    first_fix = 1.0 - 0.9**STEP
    second_fix = 1.0 - 0.999**STEP
    direction = (moment_new / first_fix / (jnp.sqrt(second_new / second_fix) + 1e-08)).astype(
        jnp.bfloat16
    )
    product = lax.dot_general(
        lax.all_gather(direction, "shard", axis=0, tiled=True),
        basis,
        (((1,), (1,)), ((), ())),
        preferred_element_type=jnp.float32,
    )
    update = product.astype(jnp.bfloat16)
    return (update, moment_new, second_new)


def solution(mesh):
    return jax.shard_map(
        per_device,
        mesh=mesh,
        in_specs=(
            P("dp", "shard"),
            P("dp", None, "shard"),
            P("shard", None),
            P(("dp", "shard"), None),
            P(("dp", "shard"), None),
        ),
        out_specs=(P("dp", "shard"), P(("dp", "shard"), None), P(("dp", "shard"), None)),
        check_vma=False,
    )
```

profile of v0, /device:TPU:1, one launch (start us, length us, event | category | flops | bytes accessed | tf_op | source)
XLA Modules:
  0.0 658.6 jit_solution(13590968074573649992)
XLA Ops:
  7.2 0.0 copy-start
  7.2 0.0 reduce-scatter.4.cloned.1.call-start
  7.2 1.6 fusion.3
  8.9 159.5 %all-reduce.1 = bf16[512,1024]{1,0:T(8,128)(2,1)} all-reduce(f32[512,1024]{1,0:T(8,128)S(1)} %fusion.3), channel_id=1, replica_groups=mesh['dp'=24,'shard'=32] {'shard'}, use_global_device_ids=true, to_apply=%region_0.0 | all-reduce | flops 524288 | bytes 3145728 | tf_op jit(solution)/shard_map/psum | solution.py:18
  168.4 0.0 copy-done
  168.4 3.9 convolution_bitcast_fusion
  172.3 3.6 copy.20
  175.8 0.0 copy-start.2
  175.8 0.0 copy-start.3
  175.9 0.0 copy-start.1
  175.9 0.0 reduce-scatter.4.cloned.1.call-update
  175.9 0.0 all-gather.2.cloned.1.call-start
  175.9 402.1 %reduce-scatter.4.cloned.1.call-done = f32[32,1024]{1,0:T(8,128)} async-done(((f32[768,1024]{1,0:T(8,128)}), f32[32,1024]{1,0:T(8,128)}) %reduce-scatter.4.cloned.1.call-update) | async-done | bytes 131088 | tf_op jit(solution)/shard_map/reduce_scatter | solution.py:20
  578.1 0.0 copy-done.2
  578.1 0.0 copy-done.3
  578.1 1.7 divide_convert_fusion
  579.7 0.0 all-gather.2.cloned.1.call-update
  579.7 68.9 %all-gather.2.cloned.1.call-done = bf16[1024,1024]{1,0:T(8,128)(2,1)} async-done(((bf16[32,1024]{1,0:T(8,128)(2,1)}), bf16[1024,1024]{1,0:T(8,128)(2,1)}) %all-gather.2.cloned.1.call-update) | async-done | bytes 2097168 | tf_op jit(solution)/shard_map/all_gather | solution.py:31
  648.7 0.0 copy-done.1
  648.7 3.1 convolution_convert_fusion
Async XLA Ops:
  7.2 161.2 %copy-start = (bf16[512,24,32]{0,2,1:T(8,128)(2,1)S(1)}, bf16[512,24,32]{0,2,1:T(8,128)(2,1)}, u32[]{:S(2)}) copy-start(bf16[512,24,32]{0,2,1:T(8,128)(2,1)} %param.6) | copy-start | bytes 2359300
  7.2 570.9 %reduce-scatter.4.cloned.1.call-start = ((), (), s32[]{:S(2)}) async-start(), calls=%async_computation.2 | async-start | bytes 3276800 | tf_op jit(solution)/shard_map/reduce_scatter | solution.py:20
  175.8 402.2 %copy-start.2 = (f32[32,1024]{1,0:T(8,128)S(1)}, f32[32,1024]{1,0:T(8,128)}, u32[]{:S(2)}) copy-start(f32[32,1024]{1,0:T(8,128)} %param.8) | copy-start | bytes 393220
  175.8 402.2 %copy-start.3 = (f32[32,1024]{1,0:T(8,128)S(1)}, f32[32,1024]{1,0:T(8,128)}, u32[]{:S(2)}) copy-start(f32[32,1024]{1,0:T(8,128)} %param.9) | copy-start | bytes 393220
  175.9 472.8 %copy-start.1 = (bf16[256,1024]{1,0:T(8,128)(2,1)S(1)}, bf16[256,1024]{1,0:T(8,128)(2,1)}, u32[]{:S(2)}) copy-start(bf16[256,1024]{1,0:T(8,128)(2,1)} %param.7) | copy-start | bytes 1572868
  175.9 472.8 %all-gather.2.cloned.1.call-start = ((), (), s32[]{:S(2)}) async-start(), calls=%async_computation.1 | async-start | bytes 2162688 | tf_op jit(solution)/shard_map/all_gather | solution.py:31
Sparse Core Ops, SparseCore 0:
  176.0 402.0 reduce-scatter.3
  581.1 67.5 all-gather.1
where the time goes:
time: 659 us
  waiting for transfers between devices  471 us (71%)
  blocking collectives  160 us (24%)
  between operations  14.1 us (2%)
  matrix products  8.67 us (1%)
    reduce_scatter x1, waiting for transfers between devices, per_device(): lax.psum_scatter(contract_rows(flat_hidden, projected), 'dp', scatter_dim...  402 us
    psum x1, blocking collectives, per_device(): projected = lax.psum(partial_basis, 'shard').astype(jnp.bfloat16)  160 us
    all_gather x1, waiting for transfers between devices, per_device(): lax.all_gather(direction, 'shard', axis=0, tiled=True)  68.9 us
  transfers between devices with their start and end apart: 2, of which 2 were waited for; matrix products, arithmetic and copies ran while one was open for 0% of the time, Pallas kernels for 0%

commit v1 on v0

v1 whole, which is shorter than its diff:
```python
import jax
import jax.numpy as jnp
from jax import lax
from jax.sharding import Mesh
from jax.sharding import PartitionSpec as P

STEP = 20
NAMES = ("zh", "zl", "yh", "yl", "x", "c")
SIZES = (4, 3, 2, 4, 4, 2)
BF16 = jnp.bfloat16
F32 = jnp.float32


def swap(array, axis):
    return lax.ppermute(array, axis, [(0, 1), (1, 0)])


def along_z(array, step):
    count = SIZES[0] * SIZES[1]
    return lax.ppermute(array, ("zh", "zl"), [(i, (i + step) % count) for i in range(count)])


def gather(array, axes, count):
    return lax.all_to_all(jnp.broadcast_to(array, (count,) + array.shape), axes, 0, 0)


def scatter_sum(array, axes, count, kept=1):
    rows = array.shape[0] // count
    parts = array.astype(BF16).reshape((count, rows) + array.shape[1:])
    parts = lax.all_to_all(parts, axes, 0, 0).astype(F32)
    if kept == 1:
        return jnp.sum(parts, axis=0)
    return jnp.sum(parts.reshape((count // kept, kept) + parts.shape[1:]), axis=0)


def pick(array, axis, index):
    return lax.dynamic_index_in_dim(array, index, axis, keepdims=False)


def dot(left, right, left_dim, right_dim):
    return lax.dot_general(
        left, right, (((left_dim,), (right_dim,)), ((), ())), preferred_element_type=F32
    )


def per_device(out_grad, hidden, basis, moment, second):
    n_zh, n_zl, n_yh, n_yl, n_x, n_c = SIZES
    zl, c = lax.axis_index("zl"), lax.axis_index("c")
    tokens, groups, cols = hidden.shape
    feats, rank = basis.shape
    half = rank // n_c

    both = lax.all_gather(hidden.transpose(1, 2, 0), "c")

    def half_of(index):
        return dot(out_grad, lax.dynamic_slice_in_dim(basis, index * half, half, 1), 1, 0)

    total = half_of(c) + swap(half_of(1 - c).astype(BF16), "c").astype(F32)
    rows = scatter_sum(total, ("x", "yl"), n_x * n_yl).astype(BF16)
    projected = gather(rows, ("x", "yl"), n_x * n_yl).reshape(tokens, half)

    late, projected = lax.optimization_barrier((basis, projected))
    wide = lax.all_gather(late, ("x", "c"), tiled=True)

    both = both.reshape(n_c, n_zh, n_zl, n_yh, cols, tokens)

    def groups_of(step):
        left = pick(both, 2, (zl + step) % n_zl).transpose(1, 2, 0, 3, 4)
        return dot(left.reshape(-1, tokens), projected, 1, 0)

    up = along_z(groups_of(1).astype(BF16), 1)
    down = along_z(groups_of(2).astype(BF16), -1)
    low = groups_of(0) + up.astype(F32) + down.astype(F32)
    low = scatter_sum(low, ("zh", "yh", "c"), n_zh * n_yh * n_c, n_c)
    lowrank = low.transpose(1, 0, 2).reshape(cols, rank)

    moment_new = 0.9 * moment + 0.1 * lowrank
    second_new = 0.999 * second + 0.001 * lowrank * lowrank
    first_fix = 1.0 - 0.9**STEP
    second_fix = 1.0 - 0.999**STEP
    direction = (moment_new / first_fix / (jnp.sqrt(second_new / second_fix) + 1e-08)).astype(BF16)

    rows = gather(direction, "yl", n_yl).reshape(n_yl * cols, rank)
    update = dot(rows, wide, 1, 1).astype(BF16).reshape(n_yl * cols, n_x * n_c, feats)
    update = lax.all_to_all(update.transpose(1, 0, 2), ("x", "c"), 0, 0)
    update = update.reshape(n_x * n_c, n_yl, cols, feats).transpose(1, 0, 2, 3)
    return (update.reshape(-1, feats), moment_new, second_new)


def solution(mesh):
    fine = Mesh(mesh.devices.reshape(SIZES), NAMES)
    dp, shard = NAMES[:3], NAMES[3:]
    every = P(NAMES, None)
    return jax.shard_map(
        per_device,
        mesh=fine,
        in_specs=(P(dp, shard), P(dp, None, shard), P(shard, None), every, every),
        out_specs=(P(dp, shard), every, every),
        check_vma=False,
    )
```

time: 659 us -> 163 us (0.25)
  the two profiles are of different devices: /device:TPU:1 before, /device:TPU:64 now
where the time goes in v1:
time: 163 us; the launch traced here: 162 us
  blocking collectives  88 us (54%)
  waiting for transfers between devices  28.9 us (18%)
  starting transfers between devices  18.3 us (11%)
  between operations  14.3 us (9%)
  matrix products  8.31 us (5%)
  local copies, waits for them, and re-layouts  3.49 us (2%)
    all_to_all x1, blocking collectives, scatter_sum(): parts = lax.all_to_all(parts, axes, 0, 0).astype(F32)  43.6 us
    all_to_all x2, blocking collectives, gather(): lax.all_to_all(jnp.broadcast_to(array, (count,) + array.shape), axes, 0, 0)  31.2 us
    all_to_all x1, waiting for transfers between devices, scatter_sum(): parts = lax.all_to_all(parts, axes, 0, 0).astype(F32)  16 us
    all_to_all x1, blocking collectives, per_device(): update = lax.all_to_all(update.transpose(1, 0, 2), ('x', 'c'), 0, 0)  13.2 us
    ppermute x2, waiting for transfers between devices, along_z(): lax.ppermute(array, ('zh', 'zl'), [(i, (i + step) % count) for i in range...  10.3 us
    ppermute x2, starting transfers between devices, along_z(): lax.ppermute(array, ('zh', 'zl'), [(i, (i + step) % count) for i in range...  8.84 us
    dot_general x6, matrix products, dot(): lax.dot_general(left, right, (((left_dim,), (right_dim,)), ((), ())), pre...  8.31 us
    all_to_all x1, starting transfers between devices, scatter_sum(): parts = lax.all_to_all(parts, axes, 0, 0).astype(F32)  7.44 us
  transfers between devices with their start and end apart: 6, of which 4 were waited for; matrix products, arithmetic and copies ran while one was open for 2% of the time, Pallas kernels for 0%

profile of v1, /device:TPU:64, one launch (start us, length us, event | category | flops | bytes accessed | tf_op | source)
XLA Modules:
  0.0 162.2 jit_solution(3715819870170417972)
XLA Ops:
  7.2 0.9 copy-done
  8.1 1.2 fusion
  9.4 1.9 %collective-permute-start = (bf16[512,512]{1,0:T(8,128)(2,1)S(1)}, bf16[512,512]{1,0:T(8,128)(2,1)S(1)}, u32[]{:S(2)}, u32[]{:S(2)}) collective-permute-start(bf16[512,512]{1,0:T(8,128)(2,1)S(1)} %fusion), channel_id=1, source_target_pairs={{0,1},{1,0},{2,3},{3,2},{4,5},{5,4},{6,7},{7,6},{8,9},{9,8},{10,11... | collective-permute-start | bytes 1572872 | tf_op jit(solution)/shard_map/ppermute | solution.py:15
  11.3 1.9 %collective-permute-done = bf16[512,512]{1,0:T(8,128)(2,1)S(1)} collective-permute-done((bf16[512,512]{1,0:T(8,128)(2,1)S(1)}, bf16[512,512]{1,0:T(8,128)(2,1)S(1)}, u32[]{:S(2)}, u32[]{:S(2)}) %collective-permute-start) | collective-permute-done | bytes 524320 | tf_op jit(solution)/shard_map/ppermute | solution.py:15
  13.2 2.0 %add_convert_fusion.1 = bf16[512,512]{1,0:T(8,128)(2,1)} fusion(bf16[512,512]{1,0:T(8,128)(2,1)S(1)} %collective-permute-done, bf16[512,256]{1,0:T(8,128)(2,1)S(1)} %copy-done, bf16[256,1024]{1,0:T(8,128)(2,1)} %param.7, s32[]{:T(128)S(6)} %select_n.33), kind=kOutput, calls=%fused_computation.8 | convolution fusion | flops 135004160 | bytes 1572868 | tf_op jit(solution)/shard_map/dot_general | solution.py:41
  15.2 7.4 %all-to-all-start = ((bf16[16,32,512]{2,1,0:T(8,128)(2,1)}), bf16[16,32,512]{2,1,0:T(8,128)(2,1)S(1)}, u32[]{:S(2)}, u32[]{:S(2)}) async-start(bf16[16,32,512]{2,1,0:T(8,128)(2,1)} %bitcast.7), calls=%async_computation | async-start | bytes 1048576 | tf_op jit(solution)/shard_map/all_to_all | solution.py:30
  22.7 0.7 all-gather.6.cloned.1.call-update
  23.4 16.0 %all-to-all-done = bf16[16,32,512]{2,1,0:T(8,128)(2,1)S(1)} async-done(((bf16[16,32,512]{2,1,0:T(8,128)(2,1)}), bf16[16,32,512]{2,1,0:T(8,128)(2,1)S(1)}, u32[]{:S(2)}, u32[]{:S(2)}) %all-to-all-start) | async-done | bytes 524320 | tf_op jit(solution)/shard_map/all_to_all | solution.py:30
  39.5 0.1 reduce_sum.21
  39.6 19.7 %all_to_all.25 = bf16[16,32,512]{2,1,0:T(8,128)(2,1)S(1)} all-to-all(bf16[16,32,512]{2,1,0:T(8,128)(2,1)S(1)} %broadcast_in_dim.6), channel_id=1, replica_groups=mesh['zh'=4,'zl'=3,'yh'=2,'yl'=4,'x'=4,'c'=2] {'x','yl'}, dimensions={0} | all-to-all | bytes 1048576 | tf_op jit(solution)/shard_map/all_to_all | solution.py:24
  59.4 1.5 constant_dynamic-slice_fusion.1
  61.0 0.4 convolution_convert_fusion.2
  61.4 4.3 %collective-permute-start.1 = (bf16[512,512]{1,0:T(8,128)(2,1)S(1)}, bf16[512,512]{1,0:T(8,128)(2,1)S(1)}, u32[]{:S(2)}, u32[]{:S(2)}) collective-permute-start(bf16[512,512]{1,0:T(8,128)(2,1)S(1)} %convolution_convert_fusion.2), channel_id=1, source_target_pairs={{0,64},{64,128},{128,192},{192,256},{256,320},{320,384},{384,448},... | collective-permute-start | bytes 1572872 | tf_op jit(solution)/shard_map/ppermute | solution.py:20
  65.7 0.4 convolution_convert_fusion.1
  66.1 4.6 %collective-permute-start.2 = (bf16[512,512]{1,0:T(8,128)(2,1)S(1)}, bf16[512,512]{1,0:T(8,128)(2,1)S(1)}, u32[]{:S(2)}, u32[]{:S(2)}) collective-permute-start(bf16[512,512]{1,0:T(8,128)(2,1)S(1)} %convolution_convert_fusion.1), channel_id=1, source_target_pairs={{0,704},{64,0},{128,64},{192,128},{256,192},{320,256},{384,320},{4... | collective-permute-start | bytes 1572872 | tf_op jit(solution)/shard_map/ppermute | solution.py:20
  70.8 8.4 %collective-permute-done.1 = bf16[512,512]{1,0:T(8,128)(2,1)S(1)} collective-permute-done((bf16[512,512]{1,0:T(8,128)(2,1)S(1)}, bf16[512,512]{1,0:T(8,128)(2,1)S(1)}, u32[]{:S(2)}, u32[]{:S(2)}) %collective-permute-start.1) | collective-permute-done | bytes 524320 | tf_op jit(solution)/shard_map/ppermute | solution.py:20
  79.2 1.8 %collective-permute-done.2 = bf16[512,512]{1,0:T(8,128)(2,1)S(1)} collective-permute-done((bf16[512,512]{1,0:T(8,128)(2,1)S(1)}, bf16[512,512]{1,0:T(8,128)(2,1)S(1)}, u32[]{:S(2)}, u32[]{:S(2)}) %collective-permute-start.2) | collective-permute-done | bytes 524320 | tf_op jit(solution)/shard_map/ppermute | solution.py:20
  81.0 0.5 add_convert_fusion
  81.5 43.6 %all_to_all.26 = bf16[16,32,512]{2,1,0:T(8,128)(2,1)S(1)} all-to-all(bf16[16,32,512]{2,1,0:T(8,128)(2,1)S(1)} %bitcast.58), channel_id=1, replica_groups=mesh['zh'=4,'zl'=3,'yh'=2,'yl'=4,'x'=4,'c'=2] {'zh','yh','c'}, dimensions={0} | all-to-all | bytes 1048576 | tf_op jit(solution)/shard_map/all_to_all | solution.py:30
  125.2 0.8 divide_convert_fusion
  126.0 11.6 %all_to_all.27 = bf16[4,32,1024]{2,1,0:T(8,128)(2,1)S(1)} all-to-all(bf16[4,32,1024]{2,1,0:T(8,128)(2,1)S(1)} %broadcast_in_dim.7), channel_id=1, replica_groups=mesh['zh'=4,'zl'=3,'yh'=2,'yl'=4,'x'=4,'c'=2] {'yl'}, dimensions={0} | all-to-all | bytes 524288 | tf_op jit(solution)/shard_map/all_to_all | solution.py:24
  137.6 3.7 %convolution_convert_fusion = bf16[128,2048]{1,0:T(8,128)(2,1)S(1)} fusion(bf16[128,1024]{1,0:T(8,128)(2,1)S(1)} %bitcast.65, bf16[2048,1024]{1,0:T(8,128)(2,1)} %all-gather.4.cloned.1.call-done), kind=kOutput, calls=%fused_computation | convolution fusion | flops 537133056 | bytes 4980736 | tf_op jit(solution)/shard_map/dot_general | solution.py:41
  141.3 13.2 %all_to_all.28 = bf16[8,128,256]{2,1,0:T(8,128)(2,1)S(1)} all-to-all(bf16[8,128,256]{2,1,0:T(8,128)(2,1)S(1)} %bitcast.62), channel_id=1, replica_groups=mesh['zh'=4,'zl'=3,'yh'=2,'yl'=4,'x'=4,'c'=2] {'x','c'}, dimensions={0} | all-to-all | bytes 1048576 | tf_op jit(solution)/shard_map/all_to_all | solution.py:85
  154.5 0.8 copy.27
  (18 shorter events, 0.4 us)
Async XLA Ops:
  7.2 1.0 copy-start
  9.4 3.8 %collective-permute-start = (bf16[512,512]{1,0:T(8,128)(2,1)S(1)}, bf16[512,512]{1,0:T(8,128)(2,1)S(1)}, u32[]{:S(2)}, u32[]{:S(2)}) collective-permute-start(bf16[512,512]{1,0:T(8,128)(2,1)S(1)} %fusion), channel_id=1, source_target_pairs={{0,1},{1,0},{2,3},{3,2},{4,5},{5,4},{6,7},{7,6},{8,9},{9,8},{10,11... | collective-permute-start | bytes 1572872 | tf_op jit(solution)/shard_map/ppermute | solution.py:15
  15.2 24.3 %all-to-all-start = ((bf16[16,32,512]{2,1,0:T(8,128)(2,1)}), bf16[16,32,512]{2,1,0:T(8,128)(2,1)S(1)}, u32[]{:S(2)}, u32[]{:S(2)}) async-start(bf16[16,32,512]{2,1,0:T(8,128)(2,1)} %bitcast.7), calls=%async_computation | async-start | bytes 1048576 | tf_op jit(solution)/shard_map/all_to_all | solution.py:30
  22.7 36.7 %all-gather.6.cloned.1.call-start = ((), (), s32[]{:S(2)}) async-start(), calls=%async_computation.6 | async-start | bytes 2359296 | tf_op jit(solution)/shard_map/all_gather | solution.py:53
  23.4 114.2 %all-gather.4.cloned.1.call-start = ((), (), s32[]{:S(2)}) async-start(), calls=%async_computation.5 | async-start | bytes 4718592 | tf_op jit(solution)/shard_map/all_gather | solution.py:63
  61.0 64.2 %copy-start.1 = (f32[32,1024]{1,0:T(8,128)S(1)}, f32[32,1024]{1,0:T(8,128)}, u32[]{:S(2)}) copy-start(f32[32,1024]{1,0:T(8,128)} %param.8) | copy-start | bytes 393220
  61.0 64.2 %copy-start.2 = (f32[32,1024]{1,0:T(8,128)S(1)}, f32[32,1024]{1,0:T(8,128)}, u32[]{:S(2)}) copy-start(f32[32,1024]{1,0:T(8,128)} %param.9) | copy-start | bytes 393220
  61.4 17.8 %collective-permute-start.1 = (bf16[512,512]{1,0:T(8,128)(2,1)S(1)}, bf16[512,512]{1,0:T(8,128)(2,1)S(1)}, u32[]{:S(2)}, u32[]{:S(2)}) collective-permute-start(bf16[512,512]{1,0:T(8,128)(2,1)S(1)} %convolution_convert_fusion.2), channel_id=1, source_target_pairs={{0,64},{64,128},{128,192},{192,256},{256,320},{320,384},{384,448},... | collective-permute-start | bytes 1572872 | tf_op jit(solution)/shard_map/ppermute | solution.py:20
  66.1 14.9 %collective-permute-start.2 = (bf16[512,512]{1,0:T(8,128)(2,1)S(1)}, bf16[512,512]{1,0:T(8,128)(2,1)S(1)}, u32[]{:S(2)}, u32[]{:S(2)}) collective-permute-start(bf16[512,512]{1,0:T(8,128)(2,1)S(1)} %convolution_convert_fusion.1), channel_id=1, source_target_pairs={{0,704},{64,0},{128,64},{192,128},{256,192},{320,256},{384,320},{4... | collective-permute-start | bytes 1572872 | tf_op jit(solution)/shard_map/ppermute | solution.py:20
Sparse Core Ops, SparseCore 0:
  25.9 24.4 all-gather.5
  59.4 41.2 all-gather.3

commit v2 on v1

--- a/solution.py
+++ b/solution.py
@@ -1,6 +1,10 @@
+import functools
+
 import jax
 import jax.numpy as jnp
 from jax import lax
+from jax.experimental import pallas as pl
+from jax.experimental.pallas import tpu as pltpu
 from jax.sharding import Mesh
 from jax.sharding import PartitionSpec as P
 
@@ -43,14 +47,45 @@
     )
 
 
+def across(array, axis, count, flip):
+    return lax.ppermute(array, axis, [(i, i ^ flip) for i in range(count)])
+
+
+def products_kernel(n_x, place, rows, *refs):
+    *weights, out = refs
+    n_c = len(weights) // n_x
+    for near in range(n_c):
+        for flip in range(n_x):
+            index = (place[0] ^ flip) * n_c + (place[1] ^ near)
+            out[index] = dot(rows[...], weights[near * n_x + flip][...], 1, 1).astype(BF16)
+
+
+def products(place, rows, weights):
+    feats = weights[0].shape[0]
+    vmem = pl.BlockSpec(memory_space=pltpu.VMEM)
+    return pl.pallas_call(
+        functools.partial(products_kernel, SIZES[4]),
+        out_shape=jax.ShapeDtypeStruct((len(weights), rows.shape[0], feats), BF16),
+        in_specs=[pl.BlockSpec(memory_space=pltpu.SMEM)] + [vmem] * (1 + len(weights)),
+        out_specs=vmem,
+        compiler_params=pltpu.CompilerParams(vmem_limit_bytes=16 * 2**20),
+        cost_estimate=pl.CostEstimate(
+            flops=2 * rows.size * feats * len(weights),
+            bytes_accessed=2 * (rows.size + (weights[0].size + rows.shape[0] * feats) * len(weights)),
+            transcendentals=0,
+        ),
+    )(place, rows, *weights)
+
+
 def per_device(out_grad, hidden, basis, moment, second):
     n_zh, n_zl, n_yh, n_yl, n_x, n_c = SIZES
-    zl, c = lax.axis_index("zl"), lax.axis_index("c")
+    zl, x, c = lax.axis_index("zl"), lax.axis_index("x"), lax.axis_index("c")
     tokens, groups, cols = hidden.shape
     feats, rank = basis.shape
     half = rank // n_c
 
-    both = lax.all_gather(hidden.transpose(1, 2, 0), "c")
+    mine = hidden.transpose(1, 2, 0)
+    theirs = swap(mine, "c")
 
     def half_of(index):
         return dot(out_grad, lax.dynamic_slice_in_dim(basis, index * half, half, 1), 1, 0)
@@ -60,8 +95,9 @@
     projected = gather(rows, ("x", "yl"), n_x * n_yl).reshape(tokens, half)
 
     late, projected = lax.optimization_barrier((basis, projected))
-    wide = lax.all_gather(late, ("x", "c"), tiled=True)
+    near = [late] + [across(late, "x", n_x, flip) for flip in range(1, n_x)]
 
+    both = jnp.stack([jnp.where(c == 0, mine, theirs), jnp.where(c == 0, theirs, mine)])
     both = both.reshape(n_c, n_zh, n_zl, n_yh, cols, tokens)
 
     def groups_of(step):
@@ -71,6 +107,8 @@
     up = along_z(groups_of(1).astype(BF16), 1)
     down = along_z(groups_of(2).astype(BF16), -1)
     low = groups_of(0) + up.astype(F32) + down.astype(F32)
+    low, near[1], near[3] = lax.optimization_barrier((low, near[1], near[3]))
+    far = [swap(part, "c") for part in near]
     low = scatter_sum(low, ("zh", "yh", "c"), n_zh * n_yh * n_c, n_c)
     lowrank = low.transpose(1, 0, 2).reshape(cols, rank)
 
@@ -81,8 +119,8 @@
     direction = (moment_new / first_fix / (jnp.sqrt(second_new / second_fix) + 1e-08)).astype(BF16)
 
     rows = gather(direction, "yl", n_yl).reshape(n_yl * cols, rank)
-    update = dot(rows, wide, 1, 1).astype(BF16).reshape(n_yl * cols, n_x * n_c, feats)
-    update = lax.all_to_all(update.transpose(1, 0, 2), ("x", "c"), 0, 0)
+    update = products(jnp.stack([x, c]).astype(jnp.int32), rows, near + far)
+    update = lax.all_to_all(update.reshape(n_x * n_c, n_yl * cols, feats), ("x", "c"), 0, 0)
     update = update.reshape(n_x * n_c, n_yl, cols, feats).transpose(1, 0, 2, 3)
     return (update.reshape(-1, feats), moment_new, second_new)
 

time: 163 us -> 155 us (0.951)
  the two profiles are of different devices: /device:TPU:64 before, /device:TPU:128 now
where the time goes in v2:
time: 155 us; the launch traced here: 154 us
  waiting for transfers between devices  69.6 us (45%)
  starting transfers between devices  56.4 us (36%)
  blocking collectives  12.9 us (8%)
  matrix products  4.45 us (3%)
  local copies, waits for them, and re-layouts  4.27 us (3%)
  Pallas kernels  2.87 us (2%)
  other arithmetic  2.39 us (2%)
    all_to_all x2, waiting for transfers between devices, scatter_sum(): parts = lax.all_to_all(parts, axes, 0, 0).astype(F32)  24.6 us
    all_to_all x2, waiting for transfers between devices, gather(): lax.all_to_all(jnp.broadcast_to(array, (count,) + array.shape), axes, 0, 0)  23.8 us
    all_to_all x2, starting transfers between devices, scatter_sum(): parts = lax.all_to_all(parts, axes, 0, 0).astype(F32)  23 us
    all_to_all x1, blocking collectives, per_device(): lax.all_to_all(update.reshape(n_x * n_c, n_yl * cols, feats), ('x', 'c'),...  12.9 us
    ppermute x6, starting transfers between devices, swap(): return lax.ppermute(array, axis, [(0, 1), (1, 0)])  12.1 us
    ppermute x3, waiting for transfers between devices, across(): return lax.ppermute(array, axis, [(i, i ^ flip) for i in range(count)])  10.4 us
    ppermute x2, waiting for transfers between devices, along_z(): lax.ppermute(array, ('zh', 'zl'), [(i, (i + step) % count) for i in range...  8.82 us
    ppermute x3, starting transfers between devices, across(): return lax.ppermute(array, axis, [(i, i ^ flip) for i in range(count)])  8 us
  transfers between devices with their start and end apart: 15, of which 9 were waited for; matrix products, arithmetic and copies ran while one was open for 4% of the time, Pallas kernels for 0%

profile of v2, /device:TPU:128, one launch (start us, length us, event | category | flops | bytes accessed | tf_op | source)
XLA Modules:
  0.0 153.8 jit_solution(8312174124945376475)
XLA Ops:
  2.8 1.9 %collective-permute-start.1 = (bf16[512,512]{1,0:T(8,128)(2,1)S(1)}, bf16[512,512]{1,0:T(8,128)(2,1)S(1)}, u32[]{:S(2)}, u32[]{:S(2)}) collective-permute-start(bf16[512,512]{1,0:T(8,128)(2,1)S(1)} %fusion), channel_id=1, source_target_pairs={{0,1},{1,0},{2,3},{3,2},{4,5},{5,4},{6,7},{7,6},{8,9},{9,8},{10,11... | collective-permute-start | bytes 1572872 | tf_op jit(solution)/shard_map/ppermute | solution.py:19
  7.7 7.6 %all-to-all-start = ((bf16[16,32,512]{2,1,0:T(8,128)(2,1)}), bf16[16,32,512]{2,1,0:T(8,128)(2,1)S(1)}, u32[]{:S(2)}, u32[]{:S(2)}) async-start(bf16[16,32,512]{2,1,0:T(8,128)(2,1)} %bitcast.10), calls=%async_computation | async-start | bytes 1048576 | tf_op jit(solution)/shard_map/all_to_all | solution.py:34
  15.3 1.9 %collective-permute-start = (bf16[24,32,512]{2,1,0:T(8,128)(2,1)S(1)}, bf16[24,32,512]{2,1,0:T(8,128)(2,1)}, u32[]{:S(2)}, u32[]{:S(2)}) collective-permute-start(bf16[24,32,512]{2,1,0:T(8,128)(2,1)S(1)} %bitcast.60), channel_id=1, source_target_pairs={{0,1},{1,0},{2,3},{3,2},{4,5},{5,4},{6,7},{7,6},{8,9},{9,8},{10,11... | collective-permute-start | bytes 2359304 | tf_op jit(solution)/shard_map/ppermute | solution.py:19
  17.3 14.9 %all-to-all-done = bf16[16,32,512]{2,1,0:T(8,128)(2,1)S(1)} async-done(((bf16[16,32,512]{2,1,0:T(8,128)(2,1)}), bf16[16,32,512]{2,1,0:T(8,128)(2,1)S(1)}, u32[]{:S(2)}, u32[]{:S(2)}) %all-to-all-start) | async-done | bytes 524320 | tf_op jit(solution)/shard_map/all_to_all | solution.py:34
  33.0 3.6 %all-to-all-start.1 = ((bf16[16,32,512]{2,1,0:T(8,128)(2,1)}), bf16[16,32,512]{2,1,0:T(8,128)(2,1)S(1)}, u32[]{:S(2)}, u32[]{:S(2)}) async-start(bf16[16,32,512]{2,1,0:T(8,128)(2,1)} %broadcast_in_dim.6), calls=%async_computation.1 | async-start | bytes 1048576 | tf_op jit(solution)/shard_map/all_to_all | solution.py:28
  38.2 14.7 %all-to-all-done.1 = bf16[16,32,512]{2,1,0:T(8,128)(2,1)S(1)} async-done(((bf16[16,32,512]{2,1,0:T(8,128)(2,1)}), bf16[16,32,512]{2,1,0:T(8,128)(2,1)S(1)}, u32[]{:S(2)}, u32[]{:S(2)}) %all-to-all-start.1) | async-done | bytes 524320 | tf_op jit(solution)/shard_map/all_to_all | solution.py:28
  53.4 4.3 %collective-permute-start.2 = (bf16[512,512]{1,0:T(8,128)(2,1)S(1)}, bf16[512,512]{1,0:T(8,128)(2,1)S(1)}, u32[]{:S(2)}, u32[]{:S(2)}) collective-permute-start(bf16[512,512]{1,0:T(8,128)(2,1)S(1)} %convolution_convert_fusion.1), channel_id=1, source_target_pairs={{0,64},{64,128},{128,192},{192,256},{256,320},{320,384},{384,448},... | collective-permute-start | bytes 1572872 | tf_op jit(solution)/shard_map/ppermute | solution.py:24
  58.1 1.9 %collective-permute-start.3 = (bf16[512,512]{1,0:T(8,128)(2,1)S(1)}, bf16[512,512]{1,0:T(8,128)(2,1)S(1)}, u32[]{:S(2)}, u32[]{:S(2)}) collective-permute-start(bf16[512,512]{1,0:T(8,128)(2,1)S(1)} %convolution_convert_fusion), channel_id=1, source_target_pairs={{0,704},{64,0},{128,64},{192,128},{256,192},{320,256},{384,320},{4... | collective-permute-start | bytes 1572872 | tf_op jit(solution)/shard_map/ppermute | solution.py:24
  60.0 1.9 %collective-permute-start.4 = (bf16[256,1024]{1,0:T(8,128)(2,1)S(1)}, bf16[256,1024]{1,0:T(8,128)(2,1)S(1)}, u32[]{:S(2)}, u32[]{:S(2)}) collective-permute-start(bf16[256,1024]{1,0:T(8,128)(2,1)S(1)} %copy-done.1), channel_id=1, source_target_pairs={{0,2},{2,0},{4,6},{6,4},{1,3},{3,1},{5,7},{7,5},{8,10},{10,8},{12,... | collective-permute-start | bytes 1572872 | tf_op jit(solution)/shard_map/ppermute | solution.py:51
  62.0 3.3 %collective-permute-start.5 = (bf16[256,1024]{1,0:T(8,128)(2,1)S(1)}, bf16[256,1024]{1,0:T(8,128)(2,1)S(1)}, u32[]{:S(2)}, u32[]{:S(2)}) collective-permute-start(bf16[256,1024]{1,0:T(8,128)(2,1)S(1)} %copy-done.1), channel_id=1, source_target_pairs={{0,6},{2,4},{4,2},{6,0},{1,7},{3,5},{5,3},{7,1},{8,14},{10,12},{12... | collective-permute-start | bytes 1572872 | tf_op jit(solution)/shard_map/ppermute | solution.py:51
  65.3 2.5 %collective-permute-done.2 = bf16[512,512]{1,0:T(8,128)(2,1)S(1)} collective-permute-done((bf16[512,512]{1,0:T(8,128)(2,1)S(1)}, bf16[512,512]{1,0:T(8,128)(2,1)S(1)}, u32[]{:S(2)}, u32[]{:S(2)}) %collective-permute-start.2) | collective-permute-done | bytes 524320 | tf_op jit(solution)/shard_map/ppermute | solution.py:24
  67.8 6.3 %collective-permute-done.3 = bf16[512,512]{1,0:T(8,128)(2,1)S(1)} collective-permute-done((bf16[512,512]{1,0:T(8,128)(2,1)S(1)}, bf16[512,512]{1,0:T(8,128)(2,1)S(1)}, u32[]{:S(2)}, u32[]{:S(2)}) %collective-permute-start.3) | collective-permute-done | bytes 524320 | tf_op jit(solution)/shard_map/ppermute | solution.py:24
  75.4 2.0 %collective-permute-done.5.refs_3_ = bf16[256,1024]{1,0:T(8,128)(2,1)S(1)} collective-permute-done((bf16[256,1024]{1,0:T(8,128)(2,1)S(1)}, bf16[256,1024]{1,0:T(8,128)(2,1)S(1)}, u32[]{:S(2)}, u32[]{:S(2)}) %collective-permute-start.5) | collective-permute-done | bytes 524320 | tf_op jit(solution)/shard_map/ppermute | solution.py:51
  77.4 15.5 %all-to-all-start.2 = ((bf16[16,32,512]{2,1,0:T(8,128)(2,1)}), bf16[16,32,512]{2,1,0:T(8,128)(2,1)S(1)}, u32[]{:S(2)}, u32[]{:S(2)}) async-start(bf16[16,32,512]{2,1,0:T(8,128)(2,1)} %bitcast.18), calls=%async_computation.2 | async-start | bytes 1048576 | tf_op jit(solution)/shard_map/all_to_all | solution.py:34
  92.8 2.8 %collective-permute-start.6 = (bf16[256,1024]{1,0:T(8,128)(2,1)S(1)}, bf16[256,1024]{1,0:T(8,128)(2,1)S(1)}, u32[]{:S(2)}, u32[]{:S(2)}) collective-permute-start(bf16[256,1024]{1,0:T(8,128)(2,1)S(1)} %copy-done.1), channel_id=1, source_target_pairs={{0,4},{2,6},{4,0},{6,2},{1,5},{3,7},{5,1},{7,3},{8,12},{10,14},{12... | collective-permute-start | bytes 1572872 | tf_op jit(solution)/shard_map/ppermute | solution.py:51
  95.6 2.1 %collective-permute-start.7 = (bf16[256,1024]{1,0:T(8,128)(2,1)S(1)}, bf16[256,1024]{1,0:T(8,128)(2,1)S(1)}, u32[]{:S(2)}, u32[]{:S(2)}) collective-permute-start(bf16[256,1024]{1,0:T(8,128)(2,1)S(1)} %copy-done.1), channel_id=1, source_target_pairs={{0,1},{1,0},{2,3},{3,2},{4,5},{5,4},{6,7},{7,6},{8,9},{9,8},{10,11... | collective-permute-start | bytes 1572872 | tf_op jit(solution)/shard_map/ppermute | solution.py:19
  97.7 2.3 %collective-permute-start.10 = (bf16[256,1024]{1,0:T(8,128)(2,1)S(1)}, bf16[256,1024]{1,0:T(8,128)(2,1)}, u32[]{:S(2)}, u32[]{:S(2)}) collective-permute-start(bf16[256,1024]{1,0:T(8,128)(2,1)S(1)} %collective-permute-done.5.refs_3_), channel_id=1, source_target_pairs={{0,1},{1,0},{2,3},{3,2},{4,5},{5,4},{6,7},{7,6},{8,9},{9,8},{10,11... | collective-permute-start | bytes 1572872 | tf_op jit(solution)/shard_map/ppermute | solution.py:19
  100.0 2.1 %collective-permute-start.8 = (bf16[256,1024]{1,0:T(8,128)(2,1)S(1)}, bf16[256,1024]{1,0:T(8,128)(2,1)}, u32[]{:S(2)}, u32[]{:S(2)}) collective-permute-start(bf16[256,1024]{1,0:T(8,128)(2,1)S(1)} %collective-permute-done.4.refs_1_), channel_id=1, source_target_pairs={{0,1},{1,0},{2,3},{3,2},{4,5},{5,4},{6,7},{7,6},{8,9},{9,8},{10,11... | collective-permute-start | bytes 1572872 | tf_op jit(solution)/shard_map/ppermute | solution.py:19
  102.0 8.5 %collective-permute-done.6.refs_2_ = bf16[256,1024]{1,0:T(8,128)(2,1)S(1)} collective-permute-done((bf16[256,1024]{1,0:T(8,128)(2,1)S(1)}, bf16[256,1024]{1,0:T(8,128)(2,1)S(1)}, u32[]{:S(2)}, u32[]{:S(2)}) %collective-permute-start.6) | collective-permute-done | bytes 524320 | tf_op jit(solution)/shard_map/ppermute | solution.py:51
  112.4 9.8 %all-to-all-done.2 = bf16[16,32,512]{2,1,0:T(8,128)(2,1)S(1)} async-done(((bf16[16,32,512]{2,1,0:T(8,128)(2,1)}), bf16[16,32,512]{2,1,0:T(8,128)(2,1)S(1)}, u32[]{:S(2)}, u32[]{:S(2)}) %all-to-all-start.2) | async-done | bytes 524320 | tf_op jit(solution)/shard_map/all_to_all | solution.py:34
  124.6 3.4 %all-to-all-start.3 = ((bf16[4,32,1024]{2,1,0:T(8,128)(2,1)}), bf16[4,32,1024]{2,1,0:T(8,128)(2,1)S(1)}, u32[]{:S(2)}, u32[]{:S(2)}) async-start(bf16[4,32,1024]{2,1,0:T(8,128)(2,1)} %broadcast_in_dim.7), calls=%async_computation.3 | async-start | bytes 524288 | tf_op jit(solution)/shard_map/all_to_all | solution.py:28
  128.1 9.1 %all-to-all-done.3 = bf16[4,32,1024]{2,1,0:T(8,128)(2,1)S(1)} async-done(((bf16[4,32,1024]{2,1,0:T(8,128)(2,1)}), bf16[4,32,1024]{2,1,0:T(8,128)(2,1)S(1)}, u32[]{:S(2)}, u32[]{:S(2)}) %all-to-all-start.3) | async-done | bytes 262176 | tf_op jit(solution)/shard_map/all_to_all | solution.py:28
  137.2 2.9 %shard_map.76 = bf16[8,128,256]{2,1,0:T(8,128)(2,1)S(1)} custom-call(s32[2]{0:T(128)S(1)} %pad_add_fusion.place, bf16[128,1024]{1,0:T(8,128)(2,1)S(1)} %bitcast.49, bf16[256,1024]{1,0:T(8,128)(2,1)S(1)} %copy-done.1, bf16[256,1024]{1,0:T(8,128)(2,1)S(1)} %collective-permute-done.4.refs_1_, bf16[256,1024]{1,0:T(8,128)(2,1)S(1)} %collective-permute-done.6.refs_2_, ...), custom_call_target="tpu_custom_call" | custom-call | flops 536870912 | bytes 4980736 | tf_op jit(solution)/shard_map/pallas_call | solution.py:66
  140.1 12.9 %all_to_all.25 = bf16[8,128,256]{2,1,0:T(8,128)(2,1)S(1)} all-to-all(bf16[8,128,256]{2,1,0:T(8,128)(2,1)S(1)} %shard_map.76), channel_id=1, replica_groups=mesh['zh'=4,'zl'=3,'yh'=2,'yl'=4,'x'=4,'c'=2] {'x','c'}, dimensions={0} | all-to-all | bytes 1048576 | tf_op jit(solution)/shard_map/all_to_all | solution.py:123
  (36 shorter events, 14.9 us)
Async XLA Ops:
  0.6 1.0 copy-start
  0.6 6.0 %copy-start.1 = (bf16[256,1024]{1,0:T(8,128)(2,1)S(1)}, bf16[256,1024]{1,0:T(8,128)(2,1)}, u32[]{:S(2)}) copy-start(bf16[256,1024]{1,0:T(8,128)(2,1)} %refs_0_) | copy-start | bytes 1572868
  2.8 3.8 %collective-permute-start.1 = (bf16[512,512]{1,0:T(8,128)(2,1)S(1)}, bf16[512,512]{1,0:T(8,128)(2,1)S(1)}, u32[]{:S(2)}, u32[]{:S(2)}) collective-permute-start(bf16[512,512]{1,0:T(8,128)(2,1)S(1)} %fusion), channel_id=1, source_target_pairs={{0,1},{1,0},{2,3},{3,2},{4,5},{5,4},{6,7},{7,6},{8,9},{9,8},{10,11... | collective-permute-start | bytes 1572872 | tf_op jit(solution)/shard_map/ppermute | solution.py:19
  7.7 7.6 %copy-start.2 = (bf16[512,24,32]{0,2,1:T(8,128)(2,1)S(1)}, bf16[512,24,32]{0,2,1:T(8,128)(2,1)}, u32[]{:S(2)}) copy-start(bf16[512,24,32]{0,2,1:T(8,128)(2,1)} %param.6) | copy-start | bytes 2359300
  7.7 24.4 %all-to-all-start = ((bf16[16,32,512]{2,1,0:T(8,128)(2,1)}), bf16[16,32,512]{2,1,0:T(8,128)(2,1)S(1)}, u32[]{:S(2)}, u32[]{:S(2)}) async-start(bf16[16,32,512]{2,1,0:T(8,128)(2,1)} %bitcast.10), calls=%async_computation | async-start | bytes 1048576 | tf_op jit(solution)/shard_map/all_to_all | solution.py:34
  15.3 21.4 %collective-permute-start = (bf16[24,32,512]{2,1,0:T(8,128)(2,1)S(1)}, bf16[24,32,512]{2,1,0:T(8,128)(2,1)}, u32[]{:S(2)}, u32[]{:S(2)}) collective-permute-start(bf16[24,32,512]{2,1,0:T(8,128)(2,1)S(1)} %bitcast.60), channel_id=1, source_target_pairs={{0,1},{1,0},{2,3},{3,2},{4,5},{5,4},{6,7},{7,6},{8,9},{9,8},{10,11... | collective-permute-start | bytes 2359304 | tf_op jit(solution)/shard_map/ppermute | solution.py:19
  33.0 19.9 %all-to-all-start.1 = ((bf16[16,32,512]{2,1,0:T(8,128)(2,1)}), bf16[16,32,512]{2,1,0:T(8,128)(2,1)S(1)}, u32[]{:S(2)}, u32[]{:S(2)}) async-start(bf16[16,32,512]{2,1,0:T(8,128)(2,1)} %broadcast_in_dim.6), calls=%async_computation.1 | async-start | bytes 1048576 | tf_op jit(solution)/shard_map/all_to_all | solution.py:28
  53.4 14.5 %collective-permute-start.2 = (bf16[512,512]{1,0:T(8,128)(2,1)S(1)}, bf16[512,512]{1,0:T(8,128)(2,1)S(1)}, u32[]{:S(2)}, u32[]{:S(2)}) collective-permute-start(bf16[512,512]{1,0:T(8,128)(2,1)S(1)} %convolution_convert_fusion.1), channel_id=1, source_target_pairs={{0,64},{64,128},{128,192},{192,256},{256,320},{320,384},{384,448},... | collective-permute-start | bytes 1572872 | tf_op jit(solution)/shard_map/ppermute | solution.py:24
  58.1 16.0 %collective-permute-start.3 = (bf16[512,512]{1,0:T(8,128)(2,1)S(1)}, bf16[512,512]{1,0:T(8,128)(2,1)S(1)}, u32[]{:S(2)}, u32[]{:S(2)}) collective-permute-start(bf16[512,512]{1,0:T(8,128)(2,1)S(1)} %convolution_convert_fusion), channel_id=1, source_target_pairs={{0,704},{64,0},{128,64},{192,128},{256,192},{320,256},{384,320},{4... | collective-permute-start | bytes 1572872 | tf_op jit(solution)/shard_map/ppermute | solution.py:24
  60.0 15.4 %collective-permute-start.4 = (bf16[256,1024]{1,0:T(8,128)(2,1)S(1)}, bf16[256,1024]{1,0:T(8,128)(2,1)S(1)}, u32[]{:S(2)}, u32[]{:S(2)}) collective-permute-start(bf16[256,1024]{1,0:T(8,128)(2,1)S(1)} %copy-done.1), channel_id=1, source_target_pairs={{0,2},{2,0},{4,6},{6,4},{1,3},{3,1},{5,7},{7,5},{8,10},{10,8},{12,... | collective-permute-start | bytes 1572872 | tf_op jit(solution)/shard_map/ppermute | solution.py:51
  62.0 15.4 %collective-permute-start.5 = (bf16[256,1024]{1,0:T(8,128)(2,1)S(1)}, bf16[256,1024]{1,0:T(8,128)(2,1)S(1)}, u32[]{:S(2)}, u32[]{:S(2)}) collective-permute-start(bf16[256,1024]{1,0:T(8,128)(2,1)S(1)} %copy-done.1), channel_id=1, source_target_pairs={{0,6},{2,4},{4,2},{6,0},{1,7},{3,5},{5,3},{7,1},{8,14},{10,12},{12... | collective-permute-start | bytes 1572872 | tf_op jit(solution)/shard_map/ppermute | solution.py:51
  77.4 44.9 %copy-start.3 = (f32[32,1024]{1,0:T(8,128)S(1)}, f32[32,1024]{1,0:T(8,128)}, u32[]{:S(2)}) copy-start(f32[32,1024]{1,0:T(8,128)} %param.8) | copy-start | bytes 393220
  77.4 44.8 %all-to-all-start.2 = ((bf16[16,32,512]{2,1,0:T(8,128)(2,1)}), bf16[16,32,512]{2,1,0:T(8,128)(2,1)S(1)}, u32[]{:S(2)}, u32[]{:S(2)}) async-start(bf16[16,32,512]{2,1,0:T(8,128)(2,1)} %bitcast.18), calls=%async_computation.2 | async-start | bytes 1048576 | tf_op jit(solution)/shard_map/all_to_all | solution.py:34
  92.8 17.7 %collective-permute-start.6 = (bf16[256,1024]{1,0:T(8,128)(2,1)S(1)}, bf16[256,1024]{1,0:T(8,128)(2,1)S(1)}, u32[]{:S(2)}, u32[]{:S(2)}) collective-permute-start(bf16[256,1024]{1,0:T(8,128)(2,1)S(1)} %copy-done.1), channel_id=1, source_target_pairs={{0,4},{2,6},{4,0},{6,2},{1,5},{3,7},{5,1},{7,3},{8,12},{10,14},{12... | collective-permute-start | bytes 1572872 | tf_op jit(solution)/shard_map/ppermute | solution.py:51
  95.6 32.5 %collective-permute-start.7 = (bf16[256,1024]{1,0:T(8,128)(2,1)S(1)}, bf16[256,1024]{1,0:T(8,128)(2,1)S(1)}, u32[]{:S(2)}, u32[]{:S(2)}) collective-permute-start(bf16[256,1024]{1,0:T(8,128)(2,1)S(1)} %copy-done.1), channel_id=1, source_target_pairs={{0,1},{1,0},{2,3},{3,2},{4,5},{5,4},{6,7},{7,6},{8,9},{9,8},{10,11... | collective-permute-start | bytes 1572872 | tf_op jit(solution)/shard_map/ppermute | solution.py:19
  97.7 30.4 %collective-permute-start.10 = (bf16[256,1024]{1,0:T(8,128)(2,1)S(1)}, bf16[256,1024]{1,0:T(8,128)(2,1)}, u32[]{:S(2)}, u32[]{:S(2)}) collective-permute-start(bf16[256,1024]{1,0:T(8,128)(2,1)S(1)} %collective-permute-done.5.refs_3_), channel_id=1, source_target_pairs={{0,1},{1,0},{2,3},{3,2},{4,5},{5,4},{6,7},{7,6},{8,9},{9,8},{10,11... | collective-permute-start | bytes 1572872 | tf_op jit(solution)/shard_map/ppermute | solution.py:19
  100.0 28.1 %collective-permute-start.8 = (bf16[256,1024]{1,0:T(8,128)(2,1)S(1)}, bf16[256,1024]{1,0:T(8,128)(2,1)}, u32[]{:S(2)}, u32[]{:S(2)}) collective-permute-start(bf16[256,1024]{1,0:T(8,128)(2,1)S(1)} %collective-permute-done.4.refs_1_), channel_id=1, source_target_pairs={{0,1},{1,0},{2,3},{3,2},{4,5},{5,4},{6,7},{7,6},{8,9},{9,8},{10,11... | collective-permute-start | bytes 1572872 | tf_op jit(solution)/shard_map/ppermute | solution.py:19
  110.5 17.6 %collective-permute-start.9 = (bf16[256,1024]{1,0:T(8,128)(2,1)S(1)}, bf16[256,1024]{1,0:T(8,128)(2,1)}, u32[]{:S(2)}, u32[]{:S(2)}) collective-permute-start(bf16[256,1024]{1,0:T(8,128)(2,1)S(1)} %collective-permute-done.6.refs_2_), channel_id=1, source_target_pairs={{0,1},{1,0},{2,3},{3,2},{4,5},{5,4},{6,7},{7,6},{8,9},{9,8},{10,11... | collective-permute-start | bytes 1572872 | tf_op jit(solution)/shard_map/ppermute | solution.py:19
  122.2 0.9 copy-start.4
  124.6 12.6 %all-to-all-start.3 = ((bf16[4,32,1024]{2,1,0:T(8,128)(2,1)}), bf16[4,32,1024]{2,1,0:T(8,128)(2,1)S(1)}, u32[]{:S(2)}, u32[]{:S(2)}) async-start(bf16[4,32,1024]{2,1,0:T(8,128)(2,1)} %broadcast_in_dim.7), calls=%async_computation.3 | async-start | bytes 524288 | tf_op jit(solution)/shard_map/all_to_all | solution.py:28

commit v3 on v2

--- a/solution.py
+++ b/solution.py
@@ -51,30 +51,35 @@
     return lax.ppermute(array, axis, [(i, i ^ flip) for i in range(count)])
 
 
-def products_kernel(n_x, place, rows, *refs):
+def products_kernel(parts, place, own, other, *refs):
     *weights, out = refs
-    n_c = len(weights) // n_x
-    for near in range(n_c):
-        for flip in range(n_x):
-            index = (place[0] ^ flip) * n_c + (place[1] ^ near)
-            out[index] = dot(rows[...], weights[near * n_x + flip][...], 1, 1).astype(BF16)
+    for flip, count in enumerate(parts):
+        at = 0
+        for _ in range(count):
+            weight = weights.pop(0)
+            feats = slice(at, at + weight.shape[0])
+            at = feats.stop
+            for far, rows in enumerate((own, other)):
+                product = dot(rows[...], weight[...], 1, 1)
+                out[place[0] ^ flip, place[1] ^ far, :, feats] = product.astype(BF16)
 
 
-def products(place, rows, weights):
-    feats = weights[0].shape[0]
+def products(place, own, other, weights):
+    rows, feats = own.shape[0], weights[0][0].shape[0]
+    parts = [len(group) for group in weights]
     vmem = pl.BlockSpec(memory_space=pltpu.VMEM)
     return pl.pallas_call(
-        functools.partial(products_kernel, SIZES[4]),
-        out_shape=jax.ShapeDtypeStruct((len(weights), rows.shape[0], feats), BF16),
-        in_specs=[pl.BlockSpec(memory_space=pltpu.SMEM)] + [vmem] * (1 + len(weights)),
+        functools.partial(products_kernel, parts),
+        out_shape=jax.ShapeDtypeStruct((len(parts), 2, rows, feats), BF16),
+        in_specs=[pl.BlockSpec(memory_space=pltpu.SMEM)] + [vmem] * (2 + sum(parts)),
         out_specs=vmem,
         compiler_params=pltpu.CompilerParams(vmem_limit_bytes=16 * 2**20),
         cost_estimate=pl.CostEstimate(
-            flops=2 * rows.size * feats * len(weights),
-            bytes_accessed=2 * (rows.size + (weights[0].size + rows.shape[0] * feats) * len(weights)),
+            flops=4 * own.size * feats * len(parts),
+            bytes_accessed=2 * (2 * own.size + feats * (own.shape[1] + 2 * rows) * len(parts)),
             transcendentals=0,
         ),
-    )(place, rows, *weights)
+    )(place, own, other, *sum(weights, []))
 
 
 def per_device(out_grad, hidden, basis, moment, second):
@@ -95,7 +100,8 @@
     projected = gather(rows, ("x", "yl"), n_x * n_yl).reshape(tokens, half)
 
     late, projected = lax.optimization_barrier((basis, projected))
-    near = [late] + [across(late, "x", n_x, flip) for flip in range(1, n_x)]
+    near = [[late]] + [[across(late, "x", n_x, flip)] for flip in range(1, n_x - 1)]
+    near.append([across(part, "x", n_x, n_x - 1) for part in jnp.split(late, 2)])
 
     both = jnp.stack([jnp.where(c == 0, mine, theirs), jnp.where(c == 0, theirs, mine)])
     both = both.reshape(n_c, n_zh, n_zl, n_yh, cols, tokens)
@@ -107,8 +113,7 @@
     up = along_z(groups_of(1).astype(BF16), 1)
     down = along_z(groups_of(2).astype(BF16), -1)
     low = groups_of(0) + up.astype(F32) + down.astype(F32)
-    low, near[1], near[3] = lax.optimization_barrier((low, near[1], near[3]))
-    far = [swap(part, "c") for part in near]
+    low, near[1][0], near[-1][0] = lax.optimization_barrier((low, near[1][0], near[-1][0]))
     low = scatter_sum(low, ("zh", "yh", "c"), n_zh * n_yh * n_c, n_c)
     lowrank = low.transpose(1, 0, 2).reshape(cols, rank)
 
@@ -118,9 +123,11 @@
     second_fix = 1.0 - 0.999**STEP
     direction = (moment_new / first_fix / (jnp.sqrt(second_new / second_fix) + 1e-08)).astype(BF16)
 
+    direction, near[1:] = lax.optimization_barrier((direction, near[1:]))
+
     rows = gather(direction, "yl", n_yl).reshape(n_yl * cols, rank)
-    update = products(jnp.stack([x, c]).astype(jnp.int32), rows, near + far)
-    update = lax.all_to_all(update.reshape(n_x * n_c, n_yl * cols, feats), ("x", "c"), 0, 0)
+    update = products(jnp.stack([x, c]).astype(jnp.int32), rows, swap(rows, "c"), near)
+    update = lax.all_to_all(update, "x", 0, 0)
     update = update.reshape(n_x * n_c, n_yl, cols, feats).transpose(1, 0, 2, 3)
     return (update.reshape(-1, feats), moment_new, second_new)
 

time: 155 us -> 151 us (0.974)
  blocking collectives: 12.9 us -> 24.3 us
  starting transfers between devices: 56.4 us -> 49.4 us
  waiting for transfers between devices: 69.6 us -> 64.2 us
    all_to_all x2, waiting for transfers between devices: 24.6 us -> 37.4 us  [scatter_sum(): parts = lax.all_to_all(parts, axes, 0, 0).astype(F32)]
    all_to_all x1 -> x2, blocking collectives: 12.9 us -> 24.3 us  [the longest x1 12.5 us: per_device(): update = lax.all_to_all(update, 'x', 0, 0)]
    ppermute x3 -> x4, waiting for transfers between devices: 10.4 us -> 0.01 us  [across(): return lax.ppermute(array, axis, [(i, i ^ flip) for i in range(count)])]
    all_to_all x2 -> x1, waiting for transfers between devices: 23.8 us -> 14.7 us  [gather(): lax.all_to_all(jnp.broadcast_to(array, (count,) + array.shape), axes, 0, 0)]
    ppermute x6 -> x3, starting transfers between devices: 12.1 us -> 5.75 us  [swap(): return lax.ppermute(array, axis, [(0, 1), (1, 0)])]
    ppermute x3 -> x4, starting transfers between devices: 8 us -> 12 us  [across(): return lax.ppermute(array, axis, [(i, i ^ flip) for i in range(count)])]
    all_to_all x2 -> x1, starting transfers between devices: 6.98 us -> 3.57 us  [gather(): lax.all_to_all(jnp.broadcast_to(array, (count,) + array.shape), axes, 0, 0)]
    ppermute x6 -> x3, waiting for transfers between devices: 1.89 us -> 3.29 us  [swap(): return lax.ppermute(array, axis, [(0, 1), (1, 0)])]
  transfers between devices with their start and end apart: 15 -> 12, of which waited for: 9 -> 7; matrix products, arithmetic and copies ran while one was open for 4% -> 3% of each run, Pallas kernels for 0% -> 0%
where the time goes in v3:
time: 151 us
  waiting for transfers between devices  64.2 us (43%)
  starting transfers between devices  49.4 us (33%)
  blocking collectives  24.3 us (16%)
  matrix products  4.45 us (3%)
  local copies, waits for them, and re-layouts  2.81 us (2%)
  other arithmetic  2.39 us (2%)
  Pallas kernels  1.98 us (1%)
    all_to_all x2, waiting for transfers between devices, scatter_sum(): parts = lax.all_to_all(parts, axes, 0, 0).astype(F32)  37.4 us
    all_to_all x2, starting transfers between devices, scatter_sum(): parts = lax.all_to_all(parts, axes, 0, 0).astype(F32)  21.9 us
    all_to_all x1, waiting for transfers between devices, gather(): lax.all_to_all(jnp.broadcast_to(array, (count,) + array.shape), axes, 0, 0)  14.7 us
    all_to_all x1, blocking collectives, per_device(): update = lax.all_to_all(update, 'x', 0, 0)  12.5 us
    ppermute x4, starting transfers between devices, across(): return lax.ppermute(array, axis, [(i, i ^ flip) for i in range(count)])  12 us
    all_to_all x1, blocking collectives, gather(): lax.all_to_all(jnp.broadcast_to(array, (count,) + array.shape), axes, 0, 0)  11.8 us
    ppermute x2, waiting for transfers between devices, along_z(): lax.ppermute(array, ('zh', 'zl'), [(i, (i + step) % count) for i in range...  8.77 us
    ppermute x2, starting transfers between devices, along_z(): lax.ppermute(array, ('zh', 'zl'), [(i, (i + step) % count) for i in range...  6.21 us
  transfers between devices with their start and end apart: 12, of which 7 were waited for; matrix products, arithmetic and copies ran while one was open for 3% of the time, Pallas kernels for 0%

profile of v3, /device:TPU:128, one launch (start us, length us, event | category | flops | bytes accessed | tf_op | source)
XLA Modules:
  0.0 150.5 jit_solution(16368527780020889515)
XLA Ops:
  2.8 1.9 %collective-permute-start.1 = (bf16[512,512]{1,0:T(8,128)(2,1)S(1)}, bf16[512,512]{1,0:T(8,128)(2,1)S(1)}, u32[]{:S(2)}, u32[]{:S(2)}) collective-permute-start(bf16[512,512]{1,0:T(8,128)(2,1)S(1)} %fusion), channel_id=1, source_target_pairs={{0,1},{1,0},{2,3},{3,2},{4,5},{5,4},{6,7},{7,6},{8,9},{9,8},{10,11... | collective-permute-start | bytes 1572872 | tf_op jit(solution)/shard_map/ppermute | solution.py:19
  4.8 1.9 %collective-permute-done.1 = bf16[512,512]{1,0:T(8,128)(2,1)S(1)} collective-permute-done((bf16[512,512]{1,0:T(8,128)(2,1)S(1)}, bf16[512,512]{1,0:T(8,128)(2,1)S(1)}, u32[]{:S(2)}, u32[]{:S(2)}) %collective-permute-start.1) | collective-permute-done | bytes 524320 | tf_op jit(solution)/shard_map/ppermute | solution.py:19
  7.7 7.6 %all-to-all-start = ((bf16[16,32,512]{2,1,0:T(8,128)(2,1)}), bf16[16,32,512]{2,1,0:T(8,128)(2,1)S(1)}, u32[]{:S(2)}, u32[]{:S(2)}) async-start(bf16[16,32,512]{2,1,0:T(8,128)(2,1)} %bitcast.10), calls=%async_computation | async-start | bytes 1048576 | tf_op jit(solution)/shard_map/all_to_all | solution.py:34
  15.3 1.9 %collective-permute-start = (bf16[24,32,512]{2,1,0:T(8,128)(2,1)S(1)}, bf16[24,32,512]{2,1,0:T(8,128)(2,1)}, u32[]{:S(2)}, u32[]{:S(2)}) collective-permute-start(bf16[24,32,512]{2,1,0:T(8,128)(2,1)S(1)} %bitcast.61), channel_id=1, source_target_pairs={{0,1},{1,0},{2,3},{3,2},{4,5},{5,4},{6,7},{7,6},{8,9},{9,8},{10,11... | collective-permute-start | bytes 2359304 | tf_op jit(solution)/shard_map/ppermute | solution.py:19
  17.3 14.9 %all-to-all-done = bf16[16,32,512]{2,1,0:T(8,128)(2,1)S(1)} async-done(((bf16[16,32,512]{2,1,0:T(8,128)(2,1)}), bf16[16,32,512]{2,1,0:T(8,128)(2,1)S(1)}, u32[]{:S(2)}, u32[]{:S(2)}) %all-to-all-start) | async-done | bytes 524320 | tf_op jit(solution)/shard_map/all_to_all | solution.py:34
  33.0 3.6 %all-to-all-start.1 = ((bf16[16,32,512]{2,1,0:T(8,128)(2,1)}), bf16[16,32,512]{2,1,0:T(8,128)(2,1)S(1)}, u32[]{:S(2)}, u32[]{:S(2)}) async-start(bf16[16,32,512]{2,1,0:T(8,128)(2,1)} %broadcast_in_dim.6), calls=%async_computation.1 | async-start | bytes 1048576 | tf_op jit(solution)/shard_map/all_to_all | solution.py:28
  36.7 1.2 broadcast_select_fusion
  38.2 14.7 %all-to-all-done.1 = bf16[16,32,512]{2,1,0:T(8,128)(2,1)S(1)} async-done(((bf16[16,32,512]{2,1,0:T(8,128)(2,1)}), bf16[16,32,512]{2,1,0:T(8,128)(2,1)S(1)}, u32[]{:S(2)}, u32[]{:S(2)}) %all-to-all-start.1) | async-done | bytes 524320 | tf_op jit(solution)/shard_map/all_to_all | solution.py:28
  53.4 4.3 %collective-permute-start.2 = (bf16[512,512]{1,0:T(8,128)(2,1)S(1)}, bf16[512,512]{1,0:T(8,128)(2,1)S(1)}, u32[]{:S(2)}, u32[]{:S(2)}) collective-permute-start(bf16[512,512]{1,0:T(8,128)(2,1)S(1)} %convolution_convert_fusion.1), channel_id=1, source_target_pairs={{0,64},{64,128},{128,192},{192,256},{256,320},{320,384},{384,448},... | collective-permute-start | bytes 1572872 | tf_op jit(solution)/shard_map/ppermute | solution.py:24
  58.1 1.9 %collective-permute-start.3 = (bf16[512,512]{1,0:T(8,128)(2,1)S(1)}, bf16[512,512]{1,0:T(8,128)(2,1)S(1)}, u32[]{:S(2)}, u32[]{:S(2)}) collective-permute-start(bf16[512,512]{1,0:T(8,128)(2,1)S(1)} %convolution_convert_fusion), channel_id=1, source_target_pairs={{0,704},{64,0},{128,64},{192,128},{256,192},{320,256},{384,320},{4... | collective-permute-start | bytes 1572872 | tf_op jit(solution)/shard_map/ppermute | solution.py:24
  60.1 1.9 %collective-permute-start.4 = (bf16[256,1024]{1,0:T(8,128)(2,1)S(1)}, bf16[256,1024]{1,0:T(8,128)(2,1)S(1)}, u32[]{:S(2)}, u32[]{:S(2)}) collective-permute-start(bf16[256,1024]{1,0:T(8,128)(2,1)S(1)} %copy-done.1), channel_id=1, source_target_pairs={{0,2},{2,0},{4,6},{6,4},{1,3},{3,1},{5,7},{7,5},{8,10},{10,8},{12,... | collective-permute-start | bytes 1572872 | tf_op jit(solution)/shard_map/ppermute | solution.py:51
  62.0 3.3 %collective-permute-start.5 = (bf16[128,1024]{1,0:T(8,128)(2,1)S(1)}, bf16[128,1024]{1,0:T(8,128)(2,1)S(1)}, u32[]{:S(2)}, u32[]{:S(2)}) collective-permute-start(bf16[128,1024]{1,0:T(8,128)(2,1)S(1)} %get-tuple-element.32), channel_id=1, source_target_pairs={{0,6},{2,4},{4,2},{6,0},{1,7},{3,5},{5,3},{7,1},{8,14},{10,12},{12... | collective-permute-start | bytes 786440 | tf_op jit(solution)/shard_map/ppermute | solution.py:51
  65.4 2.5 %collective-permute-done.2 = bf16[512,512]{1,0:T(8,128)(2,1)S(1)} collective-permute-done((bf16[512,512]{1,0:T(8,128)(2,1)S(1)}, bf16[512,512]{1,0:T(8,128)(2,1)S(1)}, u32[]{:S(2)}, u32[]{:S(2)}) %collective-permute-start.2) | collective-permute-done | bytes 524320 | tf_op jit(solution)/shard_map/ppermute | solution.py:24
  67.8 6.3 %collective-permute-done.3 = bf16[512,512]{1,0:T(8,128)(2,1)S(1)} collective-permute-done((bf16[512,512]{1,0:T(8,128)(2,1)S(1)}, bf16[512,512]{1,0:T(8,128)(2,1)S(1)}, u32[]{:S(2)}, u32[]{:S(2)}) %collective-permute-start.3) | collective-permute-done | bytes 524320 | tf_op jit(solution)/shard_map/ppermute | solution.py:24
  74.1 1.3 convert_add_fusion
  75.4 14.3 %all-to-all-start.2 = ((bf16[16,32,512]{2,1,0:T(8,128)(2,1)}), bf16[16,32,512]{2,1,0:T(8,128)(2,1)S(1)}, u32[]{:S(2)}, u32[]{:S(2)}) async-start(bf16[16,32,512]{2,1,0:T(8,128)(2,1)} %bitcast.18), calls=%async_computation.2 | async-start | bytes 1048576 | tf_op jit(solution)/shard_map/all_to_all | solution.py:34
  89.7 2.8 %collective-permute-start.6 = (bf16[256,1024]{1,0:T(8,128)(2,1)S(1)}, bf16[256,1024]{1,0:T(8,128)(2,1)S(1)}, u32[]{:S(2)}, u32[]{:S(2)}) collective-permute-start(bf16[256,1024]{1,0:T(8,128)(2,1)S(1)} %copy-done.1), channel_id=1, source_target_pairs={{0,4},{2,6},{4,0},{6,2},{1,5},{3,7},{5,1},{7,3},{8,12},{10,14},{12... | collective-permute-start | bytes 1572872 | tf_op jit(solution)/shard_map/ppermute | solution.py:51
  92.5 4.0 %collective-permute-start.7 = (bf16[128,1024]{1,0:T(8,128)(2,1)S(1)}, bf16[128,1024]{1,0:T(8,128)(2,1)S(1)}, u32[]{:S(2)}, u32[]{:S(2)}) collective-permute-start(bf16[128,1024]{1,0:T(8,128)(2,1)S(1)} %get-tuple-element.31), channel_id=1, source_target_pairs={{0,6},{2,4},{4,2},{6,0},{1,7},{3,5},{5,3},{7,1},{8,14},{10,12},{12... | collective-permute-start | bytes 786440 | tf_op jit(solution)/shard_map/ppermute | solution.py:51
  96.5 22.6 %all-to-all-done.2 = bf16[16,32,512]{2,1,0:T(8,128)(2,1)S(1)} async-done(((bf16[16,32,512]{2,1,0:T(8,128)(2,1)}), bf16[16,32,512]{2,1,0:T(8,128)(2,1)S(1)}, u32[]{:S(2)}, u32[]{:S(2)}) %all-to-all-start.2) | async-done | bytes 524320 | tf_op jit(solution)/shard_map/all_to_all | solution.py:34
  120.0 11.8 %all_to_all.25 = bf16[4,32,1024]{2,1,0:T(8,128)(2,1)S(1)} all-to-all(bf16[4,32,1024]{2,1,0:T(8,128)(2,1)S(1)} %broadcast_in_dim.7), channel_id=1, replica_groups=mesh['zh'=4,'zl'=3,'yh'=2,'yl'=4,'x'=4,'c'=2] {'yl'}, dimensions={0} | all-to-all | bytes 524288 | tf_op jit(solution)/shard_map/all_to_all | solution.py:28
  131.8 1.9 %collective-permute-start.8 = (bf16[128,1024]{1,0:T(8,128)(2,1)S(1)}, bf16[128,1024]{1,0:T(8,128)(2,1)S(1)}, u32[]{:S(2)}, u32[]{:S(2)}) collective-permute-start(bf16[128,1024]{1,0:T(8,128)(2,1)S(1)} %bitcast.49), channel_id=1, source_target_pairs={{0,1},{1,0},{2,3},{3,2},{4,5},{5,4},{6,7},{7,6},{8,9},{9,8},{10,11... | collective-permute-start | bytes 786440 | tf_op jit(solution)/shard_map/ppermute | solution.py:19
  133.8 1.4 collective-permute-done.8.other
  135.2 2.0 %shard_map.76 = bf16[4,2,128,256]{3,2,1,0:T(8,128)(2,1)S(1)} custom-call(s32[2]{0:T(128)S(1)} %pad_add_fusion.place, bf16[128,1024]{1,0:T(8,128)(2,1)S(1)} %bitcast.50, bf16[128,1024]{1,0:T(8,128)(2,1)S(1)} %collective-permute-done.8.other, bf16[256,1024]{1,0:T(8,128)(2,1)S(1)} %copy-done.1, bf16[256,1024]{1,0:T(8,128)(2,1)S(1)} %collective-permute-done.4.refs_1_, ...), custom_call_target="tpu_custom_call" | custom-call | flops 536870912 | bytes 3145728 | tf_op jit(solution)/shard_map/pallas_call | solution.py:71
  137.2 12.5 %all_to_all.26 = bf16[4,2,128,256]{3,2,1,0:T(8,128)(2,1)S(1)} all-to-all(bf16[4,2,128,256]{3,2,1,0:T(8,128)(2,1)S(1)} %shard_map.76), channel_id=1, replica_groups=mesh['zh'=4,'zl'=3,'yh'=2,'yl'=4,'x'=4,'c'=2] {'x'}, dimensions={0} | all-to-all | bytes 1048576 | tf_op jit(solution)/shard_map/all_to_all | solution.py:130
  (32 shorter events, 7.2 us)
Async XLA Ops:
  0.6 1.0 copy-start
  0.6 6.0 %copy-start.1 = (bf16[256,1024]{1,0:T(8,128)(2,1)S(1)}, bf16[256,1024]{1,0:T(8,128)(2,1)}, u32[]{:S(2)}) copy-start(bf16[256,1024]{1,0:T(8,128)(2,1)} %refs_0_) | copy-start | bytes 1572868
  2.8 3.8 %collective-permute-start.1 = (bf16[512,512]{1,0:T(8,128)(2,1)S(1)}, bf16[512,512]{1,0:T(8,128)(2,1)S(1)}, u32[]{:S(2)}, u32[]{:S(2)}) collective-permute-start(bf16[512,512]{1,0:T(8,128)(2,1)S(1)} %fusion), channel_id=1, source_target_pairs={{0,1},{1,0},{2,3},{3,2},{4,5},{5,4},{6,7},{7,6},{8,9},{9,8},{10,11... | collective-permute-start | bytes 1572872 | tf_op jit(solution)/shard_map/ppermute | solution.py:19
  7.7 7.6 %copy-start.2 = (bf16[512,24,32]{0,2,1:T(8,128)(2,1)S(1)}, bf16[512,24,32]{0,2,1:T(8,128)(2,1)}, u32[]{:S(2)}) copy-start(bf16[512,24,32]{0,2,1:T(8,128)(2,1)} %param.6) | copy-start | bytes 2359300
  7.7 24.4 %all-to-all-start = ((bf16[16,32,512]{2,1,0:T(8,128)(2,1)}), bf16[16,32,512]{2,1,0:T(8,128)(2,1)S(1)}, u32[]{:S(2)}, u32[]{:S(2)}) async-start(bf16[16,32,512]{2,1,0:T(8,128)(2,1)} %bitcast.10), calls=%async_computation | async-start | bytes 1048576 | tf_op jit(solution)/shard_map/all_to_all | solution.py:34
  15.3 21.4 %collective-permute-start = (bf16[24,32,512]{2,1,0:T(8,128)(2,1)S(1)}, bf16[24,32,512]{2,1,0:T(8,128)(2,1)}, u32[]{:S(2)}, u32[]{:S(2)}) collective-permute-start(bf16[24,32,512]{2,1,0:T(8,128)(2,1)S(1)} %bitcast.61), channel_id=1, source_target_pairs={{0,1},{1,0},{2,3},{3,2},{4,5},{5,4},{6,7},{7,6},{8,9},{9,8},{10,11... | collective-permute-start | bytes 2359304 | tf_op jit(solution)/shard_map/ppermute | solution.py:19
  33.0 19.9 %all-to-all-start.1 = ((bf16[16,32,512]{2,1,0:T(8,128)(2,1)}), bf16[16,32,512]{2,1,0:T(8,128)(2,1)S(1)}, u32[]{:S(2)}, u32[]{:S(2)}) async-start(bf16[16,32,512]{2,1,0:T(8,128)(2,1)} %broadcast_in_dim.6), calls=%async_computation.1 | async-start | bytes 1048576 | tf_op jit(solution)/shard_map/all_to_all | solution.py:28
  53.4 14.5 %collective-permute-start.2 = (bf16[512,512]{1,0:T(8,128)(2,1)S(1)}, bf16[512,512]{1,0:T(8,128)(2,1)S(1)}, u32[]{:S(2)}, u32[]{:S(2)}) collective-permute-start(bf16[512,512]{1,0:T(8,128)(2,1)S(1)} %convolution_convert_fusion.1), channel_id=1, source_target_pairs={{0,64},{64,128},{128,192},{192,256},{256,320},{320,384},{384,448},... | collective-permute-start | bytes 1572872 | tf_op jit(solution)/shard_map/ppermute | solution.py:24
  58.1 16.0 %collective-permute-start.3 = (bf16[512,512]{1,0:T(8,128)(2,1)S(1)}, bf16[512,512]{1,0:T(8,128)(2,1)S(1)}, u32[]{:S(2)}, u32[]{:S(2)}) collective-permute-start(bf16[512,512]{1,0:T(8,128)(2,1)S(1)} %convolution_convert_fusion), channel_id=1, source_target_pairs={{0,704},{64,0},{128,64},{192,128},{256,192},{320,256},{384,320},{4... | collective-permute-start | bytes 1572872 | tf_op jit(solution)/shard_map/ppermute | solution.py:24
  60.1 15.3 %collective-permute-start.4 = (bf16[256,1024]{1,0:T(8,128)(2,1)S(1)}, bf16[256,1024]{1,0:T(8,128)(2,1)S(1)}, u32[]{:S(2)}, u32[]{:S(2)}) collective-permute-start(bf16[256,1024]{1,0:T(8,128)(2,1)S(1)} %copy-done.1), channel_id=1, source_target_pairs={{0,2},{2,0},{4,6},{6,4},{1,3},{3,1},{5,7},{7,5},{8,10},{10,8},{12,... | collective-permute-start | bytes 1572872 | tf_op jit(solution)/shard_map/ppermute | solution.py:51
  62.0 13.4 %collective-permute-start.5 = (bf16[128,1024]{1,0:T(8,128)(2,1)S(1)}, bf16[128,1024]{1,0:T(8,128)(2,1)S(1)}, u32[]{:S(2)}, u32[]{:S(2)}) collective-permute-start(bf16[128,1024]{1,0:T(8,128)(2,1)S(1)} %get-tuple-element.32), channel_id=1, source_target_pairs={{0,6},{2,4},{4,2},{6,0},{1,7},{3,5},{5,3},{7,1},{8,14},{10,12},{12... | collective-permute-start | bytes 786440 | tf_op jit(solution)/shard_map/ppermute | solution.py:51
  75.4 43.8 %copy-start.3 = (f32[32,1024]{1,0:T(8,128)S(1)}, f32[32,1024]{1,0:T(8,128)}, u32[]{:S(2)}) copy-start(f32[32,1024]{1,0:T(8,128)} %param.8) | copy-start | bytes 393220
  75.4 43.8 %copy-start.4 = (f32[32,1024]{1,0:T(8,128)S(1)}, f32[32,1024]{1,0:T(8,128)}, u32[]{:S(2)}) copy-start(f32[32,1024]{1,0:T(8,128)} %param.9) | copy-start | bytes 393220
  75.4 43.7 %all-to-all-start.2 = ((bf16[16,32,512]{2,1,0:T(8,128)(2,1)}), bf16[16,32,512]{2,1,0:T(8,128)(2,1)S(1)}, u32[]{:S(2)}, u32[]{:S(2)}) async-start(bf16[16,32,512]{2,1,0:T(8,128)(2,1)} %bitcast.18), calls=%async_computation.2 | async-start | bytes 1048576 | tf_op jit(solution)/shard_map/all_to_all | solution.py:34
  89.7 30.2 %collective-permute-start.6 = (bf16[256,1024]{1,0:T(8,128)(2,1)S(1)}, bf16[256,1024]{1,0:T(8,128)(2,1)S(1)}, u32[]{:S(2)}, u32[]{:S(2)}) collective-permute-start(bf16[256,1024]{1,0:T(8,128)(2,1)S(1)} %copy-done.1), channel_id=1, source_target_pairs={{0,4},{2,6},{4,0},{6,2},{1,5},{3,7},{5,1},{7,3},{8,12},{10,14},{12... | collective-permute-start | bytes 1572872 | tf_op jit(solution)/shard_map/ppermute | solution.py:51
  92.5 27.5 %collective-permute-start.7 = (bf16[128,1024]{1,0:T(8,128)(2,1)S(1)}, bf16[128,1024]{1,0:T(8,128)(2,1)S(1)}, u32[]{:S(2)}, u32[]{:S(2)}) collective-permute-start(bf16[128,1024]{1,0:T(8,128)(2,1)S(1)} %get-tuple-element.31), channel_id=1, source_target_pairs={{0,6},{2,4},{4,2},{6,0},{1,7},{3,5},{5,3},{7,1},{8,14},{10,12},{12... | collective-permute-start | bytes 786440 | tf_op jit(solution)/shard_map/ppermute | solution.py:51
  131.8 3.4 %collective-permute-start.8 = (bf16[128,1024]{1,0:T(8,128)(2,1)S(1)}, bf16[128,1024]{1,0:T(8,128)(2,1)S(1)}, u32[]{:S(2)}, u32[]{:S(2)}) collective-permute-start(bf16[128,1024]{1,0:T(8,128)(2,1)S(1)} %bitcast.49), channel_id=1, source_target_pairs={{0,1},{1,0},{2,3},{3,2},{4,5},{5,4},{6,7},{7,6},{8,9},{9,8},{10,11... | collective-permute-start | bytes 786440 | tf_op jit(solution)/shard_map/ppermute | solution.py:19

commit v4 on v3

--- a/solution.py
+++ b/solution.py
@@ -52,20 +52,32 @@
 
 
 def products_kernel(parts, place, own, other, *refs):
-    *weights, out = refs
-    for flip, count in enumerate(parts):
+    *weights, out, full = refs
+    half = own.shape[-1]
+    count = full.shape[1]
+    for core in range(2):
+        @pl.when(place[1] == core)
+        def _(core=core):
+            for far in range(2):
+                full[far, :, core * half : (core + 1) * half] = own[:, far].reshape(count, half)
+                full[far, :, (1 - core) * half : (2 - core) * half] = other[:, 1 - far].reshape(
+                    count, half
+                )
+
+    for flip, number in enumerate(parts):
         at = 0
-        for _ in range(count):
+        for _ in range(number):
             weight = weights.pop(0)
             feats = slice(at, at + weight.shape[0])
             at = feats.stop
-            for far, rows in enumerate((own, other)):
-                product = dot(rows[...], weight[...], 1, 1)
+            for far in range(2):
+                product = dot(full[far], weight[...], 1, 1)
                 out[place[0] ^ flip, place[1] ^ far, :, feats] = product.astype(BF16)
 
 
 def products(place, own, other, weights):
-    rows, feats = own.shape[0], weights[0][0].shape[0]
+    n_yl, _, cols, half = own.shape
+    rows, (feats, rank) = n_yl * cols, weights[0][0].shape
     parts = [len(group) for group in weights]
     vmem = pl.BlockSpec(memory_space=pltpu.VMEM)
     return pl.pallas_call(
@@ -73,10 +85,11 @@
         out_shape=jax.ShapeDtypeStruct((len(parts), 2, rows, feats), BF16),
         in_specs=[pl.BlockSpec(memory_space=pltpu.SMEM)] + [vmem] * (2 + sum(parts)),
         out_specs=vmem,
+        scratch_shapes=[pltpu.VMEM((2, rows, rank), BF16)],
         compiler_params=pltpu.CompilerParams(vmem_limit_bytes=16 * 2**20),
         cost_estimate=pl.CostEstimate(
-            flops=4 * own.size * feats * len(parts),
-            bytes_accessed=2 * (2 * own.size + feats * (own.shape[1] + 2 * rows) * len(parts)),
+            flops=4 * rows * rank * feats * len(parts),
+            bytes_accessed=2 * (2 * rows * rank + feats * (rank + 2 * rows) * len(parts)),
             transcendentals=0,
         ),
     )(place, own, other, *sum(weights, []))
@@ -103,8 +116,13 @@
     near = [[late]] + [[across(late, "x", n_x, flip)] for flip in range(1, n_x - 1)]
     near.append([across(part, "x", n_x, n_x - 1) for part in jnp.split(late, 2)])
 
-    both = jnp.stack([jnp.where(c == 0, mine, theirs), jnp.where(c == 0, theirs, mine)])
-    both = both.reshape(n_c, n_zh, n_zl, n_yh, cols, tokens)
+    both = jnp.stack([mine, theirs]).reshape(n_c, n_zh, n_zl, n_yh, cols, tokens)
+
+    def part(array, index):
+        return lax.dynamic_slice_in_dim(array, index * half, half, 1)
+
+    kept = jnp.stack([part(moment, c), part(second, c)])
+    moments = jnp.stack([kept, swap(jnp.stack([part(moment, 1 - c), part(second, 1 - c)]), "c")], axis=1)
 
     def groups_of(step):
         left = pick(both, 2, (zl + step) % n_zl).transpose(1, 2, 0, 3, 4)
@@ -114,22 +132,33 @@
     down = along_z(groups_of(2).astype(BF16), -1)
     low = groups_of(0) + up.astype(F32) + down.astype(F32)
     low, near[1][0], near[-1][0] = lax.optimization_barrier((low, near[1][0], near[-1][0]))
-    low = scatter_sum(low, ("zh", "yh", "c"), n_zh * n_yh * n_c, n_c)
-    lowrank = low.transpose(1, 0, 2).reshape(cols, rank)
+    low = scatter_sum(low, ("zh", "yh"), n_zh * n_yh)
+    lowrank = low.reshape(n_c, cols, half)
 
-    moment_new = 0.9 * moment + 0.1 * lowrank
-    second_new = 0.999 * second + 0.001 * lowrank * lowrank
+    moment_new = 0.9 * moments[0] + 0.1 * lowrank
+    second_new = 0.999 * moments[1] + 0.001 * lowrank * lowrank
     first_fix = 1.0 - 0.9**STEP
     second_fix = 1.0 - 0.999**STEP
     direction = (moment_new / first_fix / (jnp.sqrt(second_new / second_fix) + 1e-08)).astype(BF16)
 
     direction, near[1:] = lax.optimization_barrier((direction, near[1:]))
 
-    rows = gather(direction, "yl", n_yl).reshape(n_yl * cols, rank)
+    rows = gather(direction, "yl", n_yl)
+    back = swap(jnp.stack([moment_new[1], second_new[1]]), "c")
+
+    def whole(own, other):
+        return jnp.concatenate(
+            [jnp.where(c == 0, own, other), jnp.where(c == 0, other, own)], axis=1
+        )
+
     update = products(jnp.stack([x, c]).astype(jnp.int32), rows, swap(rows, "c"), near)
     update = lax.all_to_all(update, "x", 0, 0)
     update = update.reshape(n_x * n_c, n_yl, cols, feats).transpose(1, 0, 2, 3)
-    return (update.reshape(-1, feats), moment_new, second_new)
+    return (
+        update.reshape(-1, feats),
+        whole(moment_new[0], back[0]),
+        whole(second_new[0], back[1]),
+    )
 
 
 def solution(mesh):

time: 151 us -> 147 us (0.974)
  waiting for transfers between devices: 64.2 us -> 49 us
  blocking collectives: 24.3 us -> 35.5 us
    all_to_all x2 -> x1, waiting for transfers between devices: 37.4 us -> 15.7 us  [scatter_sum(): parts = lax.all_to_all(parts, axes, 0, 0).astype(F32)]
    all_to_all x1, blocking collectives: 12.5 us -> 24 us  [scatter_sum(): parts = lax.all_to_all(parts, axes, 0, 0).astype(F32)]
    all_to_all x0 -> x1, waiting for transfers between devices: none -> 8.53 us  [per_device(): update = lax.all_to_all(update, 'x', 0, 0)]
    all_to_all x2 -> x1, starting transfers between devices: 21.9 us -> 14.1 us  [scatter_sum(): parts = lax.all_to_all(parts, axes, 0, 0).astype(F32)]
    ppermute x3 -> x5, starting transfers between devices: 5.75 us -> 10.1 us  [swap(): return lax.ppermute(array, axis, [(0, 1), (1, 0)])]
    all_to_all x0 -> x1, starting transfers between devices: none -> 3.47 us  [per_device(): update = lax.all_to_all(update, 'x', 0, 0)]
    all_to_all x1, waiting for transfers between devices: 14.7 us -> 11.9 us  [gather(): lax.all_to_all(jnp.broadcast_to(array, (count,) + array.shape), axes, 0, 0)]
    ppermute x3 -> x5, waiting for transfers between devices: 3.29 us -> 4.07 us  [swap(): return lax.ppermute(array, axis, [(0, 1), (1, 0)])]
  transfers between devices with their start and end apart: 12 -> 14, of which waited for: 7 -> 7; matrix products, arithmetic and copies ran while one was open for 3% -> 2% of each run, Pallas kernels for 0% -> 2%
where the time goes in v4:
time: 147 us; the launch traced here: 146 us
  starting transfers between devices  49.4 us (34%)
  waiting for transfers between devices  49 us (33%)
  blocking collectives  35.5 us (24%)
  matrix products  3.66 us (2%)
  local copies, waits for them, and re-layouts  2.83 us (2%)
  Pallas kernels  2.82 us (2%)
  other arithmetic  1.85 us (1%)
    all_to_all x1, blocking collectives, scatter_sum(): parts = lax.all_to_all(parts, axes, 0, 0).astype(F32)  24 us
    all_to_all x1, waiting for transfers between devices, scatter_sum(): parts = lax.all_to_all(parts, axes, 0, 0).astype(F32)  15.7 us
    all_to_all x1, starting transfers between devices, scatter_sum(): parts = lax.all_to_all(parts, axes, 0, 0).astype(F32)  14.1 us
    ppermute x4, starting transfers between devices, across(): return lax.ppermute(array, axis, [(i, i ^ flip) for i in range(count)])  12 us
    all_to_all x1, waiting for transfers between devices, gather(): lax.all_to_all(jnp.broadcast_to(array, (count,) + array.shape), axes, 0, 0)  11.9 us
    all_to_all x1, blocking collectives, gather(): lax.all_to_all(jnp.broadcast_to(array, (count,) + array.shape), axes, 0, 0)  11.4 us
    ppermute x5, starting transfers between devices, swap(): return lax.ppermute(array, axis, [(0, 1), (1, 0)])  10.1 us
    ppermute x2, waiting for transfers between devices, along_z(): lax.ppermute(array, ('zh', 'zl'), [(i, (i + step) % count) for i in range...  8.77 us
  transfers between devices with their start and end apart: 14, of which 7 were waited for; matrix products, arithmetic and copies ran while one was open for 2% of the time, Pallas kernels for 2%

profile of v4, /device:TPU:128, one launch (start us, length us, event | category | flops | bytes accessed | tf_op | source)
XLA Modules:
  0.0 146.1 jit_solution(4337571621779948223)
XLA Ops:
  2.8 1.9 %collective-permute-start.2 = (bf16[512,512]{1,0:T(8,128)(2,1)S(1)}, bf16[512,512]{1,0:T(8,128)(2,1)S(1)}, u32[]{:S(2)}, u32[]{:S(2)}) collective-permute-start(bf16[512,512]{1,0:T(8,128)(2,1)S(1)} %fusion), channel_id=1, source_target_pairs={{0,1},{1,0},{2,3},{3,2},{4,5},{5,4},{6,7},{7,6},{8,9},{9,8},{10,11... | collective-permute-start | bytes 1572872 | tf_op jit(solution)/shard_map/ppermute | solution.py:19
  4.8 1.9 %collective-permute-done.2 = bf16[512,512]{1,0:T(8,128)(2,1)S(1)} collective-permute-done((bf16[512,512]{1,0:T(8,128)(2,1)S(1)}, bf16[512,512]{1,0:T(8,128)(2,1)S(1)}, u32[]{:S(2)}, u32[]{:S(2)}) %collective-permute-start.2) | collective-permute-done | bytes 524320 | tf_op jit(solution)/shard_map/ppermute | solution.py:19
  6.9 24.0 %all_to_all.25 = bf16[16,32,512]{2,1,0:T(8,128)(2,1)S(1)} all-to-all(bf16[16,32,512]{2,1,0:T(8,128)(2,1)S(1)} %bitcast.79), channel_id=1, replica_groups=mesh['zh'=4,'zl'=3,'yh'=2,'yl'=4,'x'=4,'c'=2] {'x','yl'}, dimensions={0} | all-to-all | bytes 1048576 | tf_op jit(solution)/shard_map/all_to_all | solution.py:34
  31.9 3.6 %all-to-all-start.1 = ((bf16[16,32,512]{2,1,0:T(8,128)(2,1)}), bf16[16,32,512]{2,1,0:T(8,128)(2,1)S(1)}, u32[]{:S(2)}, u32[]{:S(2)}) async-start(bf16[16,32,512]{2,1,0:T(8,128)(2,1)} %broadcast_in_dim.6), calls=%async_computation.1 | async-start | bytes 1048576 | tf_op jit(solution)/shard_map/all_to_all | solution.py:28
  35.5 1.9 %collective-permute-start.1 = (bf16[24,32,512]{2,1,0:T(8,128)(2,1)S(1)}, bf16[24,32,512]{2,1,0:T(8,128)(2,1)S(1)}, u32[]{:S(2)}, u32[]{:S(2)}) collective-permute-start(bf16[24,32,512]{2,1,0:T(8,128)(2,1)S(1)} %bitcast.80), channel_id=1, source_target_pairs={{0,1},{1,0},{2,3},{3,2},{4,5},{5,4},{6,7},{7,6},{8,9},{9,8},{10,11... | collective-permute-start | bytes 2359304 | tf_op jit(solution)/shard_map/ppermute | solution.py:19
  37.5 2.2 %collective-permute-done.1 = bf16[24,32,512]{2,1,0:T(8,128)(2,1)S(1)} collective-permute-done((bf16[24,32,512]{2,1,0:T(8,128)(2,1)S(1)}, bf16[24,32,512]{2,1,0:T(8,128)(2,1)S(1)}, u32[]{:S(2)}, u32[]{:S(2)}) %collective-permute-start.1) | collective-permute-done | bytes 786464 | tf_op jit(solution)/shard_map/ppermute | solution.py:19
  39.9 11.9 %all-to-all-done.1 = bf16[16,32,512]{2,1,0:T(8,128)(2,1)S(1)} async-done(((bf16[16,32,512]{2,1,0:T(8,128)(2,1)}), bf16[16,32,512]{2,1,0:T(8,128)(2,1)S(1)}, u32[]{:S(2)}, u32[]{:S(2)}) %all-to-all-start.1) | async-done | bytes 524320 | tf_op jit(solution)/shard_map/all_to_all | solution.py:28
  52.2 4.3 %collective-permute-start.3 = (bf16[512,512]{1,0:T(8,128)(2,1)S(1)}, bf16[512,512]{1,0:T(8,128)(2,1)S(1)}, u32[]{:S(2)}, u32[]{:S(2)}) collective-permute-start(bf16[512,512]{1,0:T(8,128)(2,1)S(1)} %convolution_convert_fusion.1), channel_id=1, source_target_pairs={{0,64},{64,128},{128,192},{192,256},{256,320},{320,384},{384,448},... | collective-permute-start | bytes 1572872 | tf_op jit(solution)/shard_map/ppermute | solution.py:24
  57.0 1.9 %collective-permute-start.4 = (bf16[512,512]{1,0:T(8,128)(2,1)S(1)}, bf16[512,512]{1,0:T(8,128)(2,1)S(1)}, u32[]{:S(2)}, u32[]{:S(2)}) collective-permute-start(bf16[512,512]{1,0:T(8,128)(2,1)S(1)} %convolution_convert_fusion), channel_id=1, source_target_pairs={{0,704},{64,0},{128,64},{192,128},{256,192},{320,256},{384,320},{4... | collective-permute-start | bytes 1572872 | tf_op jit(solution)/shard_map/ppermute | solution.py:24
  58.9 1.9 %collective-permute-start.5 = (bf16[256,1024]{1,0:T(8,128)(2,1)S(1)}, bf16[256,1024]{1,0:T(8,128)(2,1)S(1)}, u32[]{:S(2)}, u32[]{:S(2)}) collective-permute-start(bf16[256,1024]{1,0:T(8,128)(2,1)S(1)} %copy-done.1), channel_id=1, source_target_pairs={{0,2},{2,0},{4,6},{6,4},{1,3},{3,1},{5,7},{7,5},{8,10},{10,8},{12,... | collective-permute-start | bytes 1572872 | tf_op jit(solution)/shard_map/ppermute | solution.py:51
  60.9 3.3 %collective-permute-start.6 = (bf16[128,1024]{1,0:T(8,128)(2,1)S(1)}, bf16[128,1024]{1,0:T(8,128)(2,1)S(1)}, u32[]{:S(2)}, u32[]{:S(2)}) collective-permute-start(bf16[128,1024]{1,0:T(8,128)(2,1)S(1)} %get-tuple-element.30), channel_id=1, source_target_pairs={{0,6},{2,4},{4,2},{6,0},{1,7},{3,5},{5,3},{7,1},{8,14},{10,12},{12... | collective-permute-start | bytes 786440 | tf_op jit(solution)/shard_map/ppermute | solution.py:51
  64.2 2.5 %collective-permute-done.3 = bf16[512,512]{1,0:T(8,128)(2,1)S(1)} collective-permute-done((bf16[512,512]{1,0:T(8,128)(2,1)S(1)}, bf16[512,512]{1,0:T(8,128)(2,1)S(1)}, u32[]{:S(2)}, u32[]{:S(2)}) %collective-permute-start.3) | collective-permute-done | bytes 524320 | tf_op jit(solution)/shard_map/ppermute | solution.py:24
  66.7 6.3 %collective-permute-done.4 = bf16[512,512]{1,0:T(8,128)(2,1)S(1)} collective-permute-done((bf16[512,512]{1,0:T(8,128)(2,1)S(1)}, bf16[512,512]{1,0:T(8,128)(2,1)S(1)}, u32[]{:S(2)}, u32[]{:S(2)}) %collective-permute-start.4) | collective-permute-done | bytes 524320 | tf_op jit(solution)/shard_map/ppermute | solution.py:24
  74.3 14.1 %all-to-all-start.2 = ((bf16[8,64,512]{2,1,0:T(8,128)(2,1)}), bf16[8,64,512]{2,1,0:T(8,128)(2,1)S(1)}, u32[]{:S(2)}, u32[]{:S(2)}) async-start(bf16[8,64,512]{2,1,0:T(8,128)(2,1)} %bitcast.26), calls=%async_computation.2 | async-start | bytes 1048576 | tf_op jit(solution)/shard_map/all_to_all | solution.py:34
  88.4 2.8 %collective-permute-start.7 = (bf16[256,1024]{1,0:T(8,128)(2,1)S(1)}, bf16[256,1024]{1,0:T(8,128)(2,1)S(1)}, u32[]{:S(2)}, u32[]{:S(2)}) collective-permute-start(bf16[256,1024]{1,0:T(8,128)(2,1)S(1)} %copy-done.1), channel_id=1, source_target_pairs={{0,4},{2,6},{4,0},{6,2},{1,5},{3,7},{5,1},{7,3},{8,12},{10,14},{12... | collective-permute-start | bytes 1572872 | tf_op jit(solution)/shard_map/ppermute | solution.py:51
  91.2 1.9 %collective-permute-start = (f32[2,32,512]{2,1,0:T(8,128)S(1)}, f32[2,32,512]{2,1,0:T(8,128)S(1)}, u32[]{:S(2)}, u32[]{:S(2)}) collective-permute-start(f32[2,32,512]{2,1,0:T(8,128)S(1)} %pad_maximum_fusion.1), channel_id=1, source_target_pairs={{0,1},{1,0},{2,3},{3,2},{4,5},{5,4},{6,7},{7,6},{8,9},{9,8},{10,11... | collective-permute-start | bytes 393224 | tf_op jit(solution)/shard_map/ppermute | solution.py:19
  93.2 4.0 %collective-permute-start.8 = (bf16[128,1024]{1,0:T(8,128)(2,1)S(1)}, bf16[128,1024]{1,0:T(8,128)(2,1)S(1)}, u32[]{:S(2)}, u32[]{:S(2)}) collective-permute-start(bf16[128,1024]{1,0:T(8,128)(2,1)S(1)} %get-tuple-element.29), channel_id=1, source_target_pairs={{0,6},{2,4},{4,2},{6,0},{1,7},{3,5},{5,3},{7,1},{8,14},{10,12},{12... | collective-permute-start | bytes 786440 | tf_op jit(solution)/shard_map/ppermute | solution.py:51
  97.2 15.7 %all-to-all-done.2 = bf16[8,64,512]{2,1,0:T(8,128)(2,1)S(1)} async-done(((bf16[8,64,512]{2,1,0:T(8,128)(2,1)}), bf16[8,64,512]{2,1,0:T(8,128)(2,1)S(1)}, u32[]{:S(2)}, u32[]{:S(2)}) %all-to-all-start.2) | async-done | bytes 524320 | tf_op jit(solution)/shard_map/all_to_all | solution.py:34
  113.1 11.4 %all_to_all.26.own = bf16[4,2,32,512]{3,2,1,0:T(8,128)(2,1)S(1)} all-to-all(bf16[4,2,32,512]{3,2,1,0:T(8,128)(2,1)S(1)} %broadcast_in_dim.7), channel_id=1, replica_groups=mesh['zh'=4,'zl'=3,'yh'=2,'yl'=4,'x'=4,'c'=2] {'yl'}, dimensions={0} | all-to-all | bytes 524288 | tf_op jit(solution)/shard_map/all_to_all | solution.py:28
  124.6 1.9 %collective-permute-start.9 = (bf16[4,2,32,512]{3,2,1,0:T(8,128)(2,1)S(1)}, bf16[4,2,32,512]{3,2,1,0:T(8,128)(2,1)S(1)}, u32[]{:S(2)}, u32[]{:S(2)}) collective-permute-start(bf16[4,2,32,512]{3,2,1,0:T(8,128)(2,1)S(1)} %all_to_all.26.own), channel_id=1, source_target_pairs={{0,1},{1,0},{2,3},{3,2},{4,5},{5,4},{6,7},{7,6},{8,9},{9,8},{10,11... | collective-permute-start | bytes 786440 | tf_op jit(solution)/shard_map/ppermute | solution.py:19
  126.5 2.4 %collective-permute-start.10 = (f32[2,32,512]{2,1,0:T(8,128)S(1)}, f32[2,32,512]{2,1,0:T(8,128)S(1)}, u32[]{:S(2)}, u32[]{:S(2)}) collective-permute-start(f32[2,32,512]{2,1,0:T(8,128)S(1)} %pad_maximum_fusion.2), channel_id=1, source_target_pairs={{0,1},{1,0},{2,3},{3,2},{4,5},{5,4},{6,7},{7,6},{8,9},{9,8},{10,11... | collective-permute-start | bytes 393224 | tf_op jit(solution)/shard_map/ppermute | solution.py:19
  129.0 2.8 %shard_map.76 = bf16[4,2,128,256]{3,2,1,0:T(8,128)(2,1)} custom-call(s32[2]{0:T(128)S(1)} %pad_add_fusion.place, bf16[4,2,32,512]{3,2,1,0:T(8,128)(2,1)S(1)} %all_to_all.26.own, bf16[4,2,32,512]{3,2,1,0:T(8,128)(2,1)S(1)} %collective-permute-done.9.other, bf16[256,1024]{1,0:T(8,128)(2,1)S(1)} %copy-done.1, ...), custom_call_target="tpu_custom_call" | custom-call | flops 536870912 | bytes 3145728 | tf_op jit(solution)/shard_map/pallas_call | solution.py:83
  131.9 3.5 %all-to-all-start.4 = ((bf16[4,2,128,256]{3,2,1,0:T(8,128)(2,1)}), bf16[4,2,128,256]{3,2,1,0:T(8,128)(2,1)S(1)}, u32[]{:S(2)}, u32[]{:S(2)}) async-start(bf16[4,2,128,256]{3,2,1,0:T(8,128)(2,1)} %shard_map.76), calls=%async_computation.4 | async-start | bytes 1048576 | tf_op jit(solution)/shard_map/all_to_all | solution.py:155
  136.7 8.5 %all-to-all-done.4 = bf16[4,2,128,256]{3,2,1,0:T(8,128)(2,1)S(1)} async-done(((bf16[4,2,128,256]{3,2,1,0:T(8,128)(2,1)}), bf16[4,2,128,256]{3,2,1,0:T(8,128)(2,1)S(1)}, u32[]{:S(2)}, u32[]{:S(2)}) %all-to-all-start.4) | async-done | bytes 524320 | tf_op jit(solution)/shard_map/all_to_all | solution.py:155
  (43 shorter events, 8.4 us)
Async XLA Ops:
  0.6 1.0 copy-start
  0.6 6.0 %copy-start.1 = (bf16[256,1024]{1,0:T(8,128)(2,1)S(1)}, bf16[256,1024]{1,0:T(8,128)(2,1)}, u32[]{:S(2)}) copy-start(bf16[256,1024]{1,0:T(8,128)(2,1)} %refs_0_) | copy-start | bytes 1572868
  2.8 3.8 %collective-permute-start.2 = (bf16[512,512]{1,0:T(8,128)(2,1)S(1)}, bf16[512,512]{1,0:T(8,128)(2,1)S(1)}, u32[]{:S(2)}, u32[]{:S(2)}) collective-permute-start(bf16[512,512]{1,0:T(8,128)(2,1)S(1)} %fusion), channel_id=1, source_target_pairs={{0,1},{1,0},{2,3},{3,2},{4,5},{5,4},{6,7},{7,6},{8,9},{9,8},{10,11... | collective-permute-start | bytes 1572872 | tf_op jit(solution)/shard_map/ppermute | solution.py:19
  31.1 4.4 %copy-start.2 = (bf16[512,24,32]{0,2,1:T(8,128)(2,1)S(1)}, bf16[512,24,32]{0,2,1:T(8,128)(2,1)}, u32[]{:S(2)}) copy-start(bf16[512,24,32]{0,2,1:T(8,128)(2,1)} %param.6) | copy-start | bytes 2359300
  31.9 19.9 %all-to-all-start.1 = ((bf16[16,32,512]{2,1,0:T(8,128)(2,1)}), bf16[16,32,512]{2,1,0:T(8,128)(2,1)S(1)}, u32[]{:S(2)}, u32[]{:S(2)}) async-start(bf16[16,32,512]{2,1,0:T(8,128)(2,1)} %broadcast_in_dim.6), calls=%async_computation.1 | async-start | bytes 1048576 | tf_op jit(solution)/shard_map/all_to_all | solution.py:28
  35.5 4.2 %collective-permute-start.1 = (bf16[24,32,512]{2,1,0:T(8,128)(2,1)S(1)}, bf16[24,32,512]{2,1,0:T(8,128)(2,1)S(1)}, u32[]{:S(2)}, u32[]{:S(2)}) collective-permute-start(bf16[24,32,512]{2,1,0:T(8,128)(2,1)S(1)} %bitcast.80), channel_id=1, source_target_pairs={{0,1},{1,0},{2,3},{3,2},{4,5},{5,4},{6,7},{7,6},{8,9},{9,8},{10,11... | collective-permute-start | bytes 2359304 | tf_op jit(solution)/shard_map/ppermute | solution.py:19
  52.2 14.5 %collective-permute-start.3 = (bf16[512,512]{1,0:T(8,128)(2,1)S(1)}, bf16[512,512]{1,0:T(8,128)(2,1)S(1)}, u32[]{:S(2)}, u32[]{:S(2)}) collective-permute-start(bf16[512,512]{1,0:T(8,128)(2,1)S(1)} %convolution_convert_fusion.1), channel_id=1, source_target_pairs={{0,64},{64,128},{128,192},{192,256},{256,320},{320,384},{384,448},... | collective-permute-start | bytes 1572872 | tf_op jit(solution)/shard_map/ppermute | solution.py:24
  57.0 16.0 %collective-permute-start.4 = (bf16[512,512]{1,0:T(8,128)(2,1)S(1)}, bf16[512,512]{1,0:T(8,128)(2,1)S(1)}, u32[]{:S(2)}, u32[]{:S(2)}) collective-permute-start(bf16[512,512]{1,0:T(8,128)(2,1)S(1)} %convolution_convert_fusion), channel_id=1, source_target_pairs={{0,704},{64,0},{128,64},{192,128},{256,192},{320,256},{384,320},{4... | collective-permute-start | bytes 1572872 | tf_op jit(solution)/shard_map/ppermute | solution.py:24
  58.9 15.3 %collective-permute-start.5 = (bf16[256,1024]{1,0:T(8,128)(2,1)S(1)}, bf16[256,1024]{1,0:T(8,128)(2,1)S(1)}, u32[]{:S(2)}, u32[]{:S(2)}) collective-permute-start(bf16[256,1024]{1,0:T(8,128)(2,1)S(1)} %copy-done.1), channel_id=1, source_target_pairs={{0,2},{2,0},{4,6},{6,4},{1,3},{3,1},{5,7},{7,5},{8,10},{10,8},{12,... | collective-permute-start | bytes 1572872 | tf_op jit(solution)/shard_map/ppermute | solution.py:51
  60.9 13.4 %collective-permute-start.6 = (bf16[128,1024]{1,0:T(8,128)(2,1)S(1)}, bf16[128,1024]{1,0:T(8,128)(2,1)S(1)}, u32[]{:S(2)}, u32[]{:S(2)}) collective-permute-start(bf16[128,1024]{1,0:T(8,128)(2,1)S(1)} %get-tuple-element.30), channel_id=1, source_target_pairs={{0,6},{2,4},{4,2},{6,0},{1,7},{3,5},{5,3},{7,1},{8,14},{10,12},{12... | collective-permute-start | bytes 786440 | tf_op jit(solution)/shard_map/ppermute | solution.py:51
  74.3 14.1 %copy-start.3 = (f32[32,1024]{1,0:T(8,128)S(1)}, f32[32,1024]{1,0:T(8,128)}, u32[]{:S(2)}) copy-start(f32[32,1024]{1,0:T(8,128)} %param.9) | copy-start | bytes 393220
  74.3 14.1 %copy-start.4 = (f32[32,1024]{1,0:T(8,128)S(1)}, f32[32,1024]{1,0:T(8,128)}, u32[]{:S(2)}) copy-start(f32[32,1024]{1,0:T(8,128)} %param.8) | copy-start | bytes 393220
  74.3 38.6 %all-to-all-start.2 = ((bf16[8,64,512]{2,1,0:T(8,128)(2,1)}), bf16[8,64,512]{2,1,0:T(8,128)(2,1)S(1)}, u32[]{:S(2)}, u32[]{:S(2)}) async-start(bf16[8,64,512]{2,1,0:T(8,128)(2,1)} %bitcast.26), calls=%async_computation.2 | async-start | bytes 1048576 | tf_op jit(solution)/shard_map/all_to_all | solution.py:34
  88.4 24.7 %collective-permute-start.7 = (bf16[256,1024]{1,0:T(8,128)(2,1)S(1)}, bf16[256,1024]{1,0:T(8,128)(2,1)S(1)}, u32[]{:S(2)}, u32[]{:S(2)}) collective-permute-start(bf16[256,1024]{1,0:T(8,128)(2,1)S(1)} %copy-done.1), channel_id=1, source_target_pairs={{0,4},{2,6},{4,0},{6,2},{1,5},{3,7},{5,1},{7,3},{8,12},{10,14},{12... | collective-permute-start | bytes 1572872 | tf_op jit(solution)/shard_map/ppermute | solution.py:51
  91.2 21.8 %collective-permute-start = (f32[2,32,512]{2,1,0:T(8,128)S(1)}, f32[2,32,512]{2,1,0:T(8,128)S(1)}, u32[]{:S(2)}, u32[]{:S(2)}) collective-permute-start(f32[2,32,512]{2,1,0:T(8,128)S(1)} %pad_maximum_fusion.1), channel_id=1, source_target_pairs={{0,1},{1,0},{2,3},{3,2},{4,5},{5,4},{6,7},{7,6},{8,9},{9,8},{10,11... | collective-permute-start | bytes 393224 | tf_op jit(solution)/shard_map/ppermute | solution.py:19
  93.2 19.9 %collective-permute-start.8 = (bf16[128,1024]{1,0:T(8,128)(2,1)S(1)}, bf16[128,1024]{1,0:T(8,128)(2,1)S(1)}, u32[]{:S(2)}, u32[]{:S(2)}) collective-permute-start(bf16[128,1024]{1,0:T(8,128)(2,1)S(1)} %get-tuple-element.29), channel_id=1, source_target_pairs={{0,6},{2,4},{4,2},{6,0},{1,7},{3,5},{5,3},{7,1},{8,14},{10,12},{12... | collective-permute-start | bytes 786440 | tf_op jit(solution)/shard_map/ppermute | solution.py:51
  124.6 4.5 %collective-permute-start.9 = (bf16[4,2,32,512]{3,2,1,0:T(8,128)(2,1)S(1)}, bf16[4,2,32,512]{3,2,1,0:T(8,128)(2,1)S(1)}, u32[]{:S(2)}, u32[]{:S(2)}) collective-permute-start(bf16[4,2,32,512]{3,2,1,0:T(8,128)(2,1)S(1)} %all_to_all.26.own), channel_id=1, source_target_pairs={{0,1},{1,0},{2,3},{3,2},{4,5},{5,4},{6,7},{7,6},{8,9},{9,8},{10,11... | collective-permute-start | bytes 786440 | tf_op jit(solution)/shard_map/ppermute | solution.py:19
  126.5 8.8 %collective-permute-start.10 = (f32[2,32,512]{2,1,0:T(8,128)S(1)}, f32[2,32,512]{2,1,0:T(8,128)S(1)}, u32[]{:S(2)}, u32[]{:S(2)}) collective-permute-start(f32[2,32,512]{2,1,0:T(8,128)S(1)} %pad_maximum_fusion.2), channel_id=1, source_target_pairs={{0,1},{1,0},{2,3},{3,2},{4,5},{5,4},{6,7},{7,6},{8,9},{9,8},{10,11... | collective-permute-start | bytes 393224 | tf_op jit(solution)/shard_map/ppermute | solution.py:19
  131.9 13.4 %all-to-all-start.4 = ((bf16[4,2,128,256]{3,2,1,0:T(8,128)(2,1)}), bf16[4,2,128,256]{3,2,1,0:T(8,128)(2,1)S(1)}, u32[]{:S(2)}, u32[]{:S(2)}) async-start(bf16[4,2,128,256]{3,2,1,0:T(8,128)(2,1)} %shard_map.76), calls=%async_computation.4 | async-start | bytes 1048576 | tf_op jit(solution)/shard_map/all_to_all | solution.py:155

commit v5 on v4

--- a/solution.py
+++ b/solution.py
@@ -54,13 +54,14 @@
 def products_kernel(parts, place, own, other, *refs):
     *weights, out, full = refs
     half = own.shape[-1]
-    count = full.shape[1]
+    count = full.shape[0] // 2
     for core in range(2):
         @pl.when(place[1] == core)
         def _(core=core):
             for far in range(2):
-                full[far, :, core * half : (core + 1) * half] = own[:, far].reshape(count, half)
-                full[far, :, (1 - core) * half : (2 - core) * half] = other[:, 1 - far].reshape(
+                rows = slice(far * count, (far + 1) * count)
+                full[rows, core * half : (core + 1) * half] = own[:, far].reshape(count, half)
+                full[rows, (1 - core) * half : (2 - core) * half] = other[:, 1 - far].reshape(
                     count, half
                 )
 
@@ -70,9 +71,10 @@
             weight = weights.pop(0)
             feats = slice(at, at + weight.shape[0])
             at = feats.stop
+            product = dot(full[...], weight[...], 1, 1).astype(BF16)
             for far in range(2):
-                product = dot(full[far], weight[...], 1, 1)
-                out[place[0] ^ flip, place[1] ^ far, :, feats] = product.astype(BF16)
+                rows = slice(far * count, (far + 1) * count)
+                out[place[0] ^ flip, place[1] ^ far, :, feats] = product[rows]
 
 
 def products(place, own, other, weights):
@@ -85,7 +87,7 @@
         out_shape=jax.ShapeDtypeStruct((len(parts), 2, rows, feats), BF16),
         in_specs=[pl.BlockSpec(memory_space=pltpu.SMEM)] + [vmem] * (2 + sum(parts)),
         out_specs=vmem,
-        scratch_shapes=[pltpu.VMEM((2, rows, rank), BF16)],
+        scratch_shapes=[pltpu.VMEM((2 * rows, rank), BF16)],
         compiler_params=pltpu.CompilerParams(vmem_limit_bytes=16 * 2**20),
         cost_estimate=pl.CostEstimate(
             flops=4 * rows * rank * feats * len(parts),

time: 147 us -> 146 us (level)
  transfers between devices with their start and end apart: 14 -> 14, of which waited for: 7 -> 7; matrix products, arithmetic and copies ran while one was open for 2% -> 3% of each run, Pallas kernels for 2% -> 2%
where the time goes in v5:
time: 146 us
  starting transfers between devices  49.4 us (34%)
  waiting for transfers between devices  49 us (34%)
  blocking collectives  35.5 us (24%)
  matrix products  3.66 us (3%)
  local copies, waits for them, and re-layouts  2.83 us (2%)
  Pallas kernels  2.27 us (2%)
  other arithmetic  1.85 us (1%)
    all_to_all x1, blocking collectives, scatter_sum(): parts = lax.all_to_all(parts, axes, 0, 0).astype(F32)  24 us
    all_to_all x1, waiting for transfers between devices, scatter_sum(): parts = lax.all_to_all(parts, axes, 0, 0).astype(F32)  15.7 us
    all_to_all x1, starting transfers between devices, scatter_sum(): parts = lax.all_to_all(parts, axes, 0, 0).astype(F32)  14.1 us
    ppermute x4, starting transfers between devices, across(): return lax.ppermute(array, axis, [(i, i ^ flip) for i in range(count)])  12 us
    all_to_all x1, waiting for transfers between devices, gather(): lax.all_to_all(jnp.broadcast_to(array, (count,) + array.shape), axes, 0, 0)  11.9 us
    all_to_all x1, blocking collectives, gather(): lax.all_to_all(jnp.broadcast_to(array, (count,) + array.shape), axes, 0, 0)  11.4 us
    ppermute x5, starting transfers between devices, swap(): return lax.ppermute(array, axis, [(0, 1), (1, 0)])  10.1 us
    ppermute x2, waiting for transfers between devices, along_z(): lax.ppermute(array, ('zh', 'zl'), [(i, (i + step) % count) for i in range...  8.77 us
  transfers between devices with their start and end apart: 14, of which 7 were waited for; matrix products, arithmetic and copies ran while one was open for 3% of the time, Pallas kernels for 2%

profile of v5, /device:TPU:128, one launch (start us, length us, event | category | flops | bytes accessed | tf_op | source)
XLA Modules:
  0.0 145.5 jit_solution(1879729820401381854)
XLA Ops:
  2.8 1.9 %collective-permute-start.2 = (bf16[512,512]{1,0:T(8,128)(2,1)S(1)}, bf16[512,512]{1,0:T(8,128)(2,1)S(1)}, u32[]{:S(2)}, u32[]{:S(2)}) collective-permute-start(bf16[512,512]{1,0:T(8,128)(2,1)S(1)} %fusion), channel_id=1, source_target_pairs={{0,1},{1,0},{2,3},{3,2},{4,5},{5,4},{6,7},{7,6},{8,9},{9,8},{10,11... | collective-permute-start | bytes 1572872 | tf_op jit(solution)/shard_map/ppermute | solution.py:19
  4.8 1.9 %collective-permute-done.2 = bf16[512,512]{1,0:T(8,128)(2,1)S(1)} collective-permute-done((bf16[512,512]{1,0:T(8,128)(2,1)S(1)}, bf16[512,512]{1,0:T(8,128)(2,1)S(1)}, u32[]{:S(2)}, u32[]{:S(2)}) %collective-permute-start.2) | collective-permute-done | bytes 524320 | tf_op jit(solution)/shard_map/ppermute | solution.py:19
  6.9 24.0 %all_to_all.25 = bf16[16,32,512]{2,1,0:T(8,128)(2,1)S(1)} all-to-all(bf16[16,32,512]{2,1,0:T(8,128)(2,1)S(1)} %bitcast.79), channel_id=1, replica_groups=mesh['zh'=4,'zl'=3,'yh'=2,'yl'=4,'x'=4,'c'=2] {'x','yl'}, dimensions={0} | all-to-all | bytes 1048576 | tf_op jit(solution)/shard_map/all_to_all | solution.py:34
  31.9 3.6 %all-to-all-start.1 = ((bf16[16,32,512]{2,1,0:T(8,128)(2,1)}), bf16[16,32,512]{2,1,0:T(8,128)(2,1)S(1)}, u32[]{:S(2)}, u32[]{:S(2)}) async-start(bf16[16,32,512]{2,1,0:T(8,128)(2,1)} %broadcast_in_dim.6), calls=%async_computation.1 | async-start | bytes 1048576 | tf_op jit(solution)/shard_map/all_to_all | solution.py:28
  35.5 1.9 %collective-permute-start.1 = (bf16[24,32,512]{2,1,0:T(8,128)(2,1)S(1)}, bf16[24,32,512]{2,1,0:T(8,128)(2,1)S(1)}, u32[]{:S(2)}, u32[]{:S(2)}) collective-permute-start(bf16[24,32,512]{2,1,0:T(8,128)(2,1)S(1)} %bitcast.80), channel_id=1, source_target_pairs={{0,1},{1,0},{2,3},{3,2},{4,5},{5,4},{6,7},{7,6},{8,9},{9,8},{10,11... | collective-permute-start | bytes 2359304 | tf_op jit(solution)/shard_map/ppermute | solution.py:19
  37.5 2.2 %collective-permute-done.1 = bf16[24,32,512]{2,1,0:T(8,128)(2,1)S(1)} collective-permute-done((bf16[24,32,512]{2,1,0:T(8,128)(2,1)S(1)}, bf16[24,32,512]{2,1,0:T(8,128)(2,1)S(1)}, u32[]{:S(2)}, u32[]{:S(2)}) %collective-permute-start.1) | collective-permute-done | bytes 786464 | tf_op jit(solution)/shard_map/ppermute | solution.py:19
  39.9 11.9 %all-to-all-done.1 = bf16[16,32,512]{2,1,0:T(8,128)(2,1)S(1)} async-done(((bf16[16,32,512]{2,1,0:T(8,128)(2,1)}), bf16[16,32,512]{2,1,0:T(8,128)(2,1)S(1)}, u32[]{:S(2)}, u32[]{:S(2)}) %all-to-all-start.1) | async-done | bytes 524320 | tf_op jit(solution)/shard_map/all_to_all | solution.py:28
  52.2 4.3 %collective-permute-start.3 = (bf16[512,512]{1,0:T(8,128)(2,1)S(1)}, bf16[512,512]{1,0:T(8,128)(2,1)S(1)}, u32[]{:S(2)}, u32[]{:S(2)}) collective-permute-start(bf16[512,512]{1,0:T(8,128)(2,1)S(1)} %convolution_convert_fusion.1), channel_id=1, source_target_pairs={{0,64},{64,128},{128,192},{192,256},{256,320},{320,384},{384,448},... | collective-permute-start | bytes 1572872 | tf_op jit(solution)/shard_map/ppermute | solution.py:24
  57.0 1.9 %collective-permute-start.4 = (bf16[512,512]{1,0:T(8,128)(2,1)S(1)}, bf16[512,512]{1,0:T(8,128)(2,1)S(1)}, u32[]{:S(2)}, u32[]{:S(2)}) collective-permute-start(bf16[512,512]{1,0:T(8,128)(2,1)S(1)} %convolution_convert_fusion), channel_id=1, source_target_pairs={{0,704},{64,0},{128,64},{192,128},{256,192},{320,256},{384,320},{4... | collective-permute-start | bytes 1572872 | tf_op jit(solution)/shard_map/ppermute | solution.py:24
  58.9 1.9 %collective-permute-start.5 = (bf16[256,1024]{1,0:T(8,128)(2,1)S(1)}, bf16[256,1024]{1,0:T(8,128)(2,1)S(1)}, u32[]{:S(2)}, u32[]{:S(2)}) collective-permute-start(bf16[256,1024]{1,0:T(8,128)(2,1)S(1)} %copy-done.1), channel_id=1, source_target_pairs={{0,2},{2,0},{4,6},{6,4},{1,3},{3,1},{5,7},{7,5},{8,10},{10,8},{12,... | collective-permute-start | bytes 1572872 | tf_op jit(solution)/shard_map/ppermute | solution.py:51
  60.9 3.3 %collective-permute-start.6 = (bf16[128,1024]{1,0:T(8,128)(2,1)S(1)}, bf16[128,1024]{1,0:T(8,128)(2,1)S(1)}, u32[]{:S(2)}, u32[]{:S(2)}) collective-permute-start(bf16[128,1024]{1,0:T(8,128)(2,1)S(1)} %get-tuple-element.30), channel_id=1, source_target_pairs={{0,6},{2,4},{4,2},{6,0},{1,7},{3,5},{5,3},{7,1},{8,14},{10,12},{12... | collective-permute-start | bytes 786440 | tf_op jit(solution)/shard_map/ppermute | solution.py:51
  64.2 2.5 %collective-permute-done.3 = bf16[512,512]{1,0:T(8,128)(2,1)S(1)} collective-permute-done((bf16[512,512]{1,0:T(8,128)(2,1)S(1)}, bf16[512,512]{1,0:T(8,128)(2,1)S(1)}, u32[]{:S(2)}, u32[]{:S(2)}) %collective-permute-start.3) | collective-permute-done | bytes 524320 | tf_op jit(solution)/shard_map/ppermute | solution.py:24
  66.7 6.3 %collective-permute-done.4 = bf16[512,512]{1,0:T(8,128)(2,1)S(1)} collective-permute-done((bf16[512,512]{1,0:T(8,128)(2,1)S(1)}, bf16[512,512]{1,0:T(8,128)(2,1)S(1)}, u32[]{:S(2)}, u32[]{:S(2)}) %collective-permute-start.4) | collective-permute-done | bytes 524320 | tf_op jit(solution)/shard_map/ppermute | solution.py:24
  74.3 14.1 %all-to-all-start.2 = ((bf16[8,64,512]{2,1,0:T(8,128)(2,1)}), bf16[8,64,512]{2,1,0:T(8,128)(2,1)S(1)}, u32[]{:S(2)}, u32[]{:S(2)}) async-start(bf16[8,64,512]{2,1,0:T(8,128)(2,1)} %bitcast.26), calls=%async_computation.2 | async-start | bytes 1048576 | tf_op jit(solution)/shard_map/all_to_all | solution.py:34
  88.4 2.8 %collective-permute-start.7 = (bf16[256,1024]{1,0:T(8,128)(2,1)S(1)}, bf16[256,1024]{1,0:T(8,128)(2,1)S(1)}, u32[]{:S(2)}, u32[]{:S(2)}) collective-permute-start(bf16[256,1024]{1,0:T(8,128)(2,1)S(1)} %copy-done.1), channel_id=1, source_target_pairs={{0,4},{2,6},{4,0},{6,2},{1,5},{3,7},{5,1},{7,3},{8,12},{10,14},{12... | collective-permute-start | bytes 1572872 | tf_op jit(solution)/shard_map/ppermute | solution.py:51
  91.2 1.9 %collective-permute-start = (f32[2,32,512]{2,1,0:T(8,128)S(1)}, f32[2,32,512]{2,1,0:T(8,128)S(1)}, u32[]{:S(2)}, u32[]{:S(2)}) collective-permute-start(f32[2,32,512]{2,1,0:T(8,128)S(1)} %pad_maximum_fusion.1), channel_id=1, source_target_pairs={{0,1},{1,0},{2,3},{3,2},{4,5},{5,4},{6,7},{7,6},{8,9},{9,8},{10,11... | collective-permute-start | bytes 393224 | tf_op jit(solution)/shard_map/ppermute | solution.py:19
  93.2 4.0 %collective-permute-start.8 = (bf16[128,1024]{1,0:T(8,128)(2,1)S(1)}, bf16[128,1024]{1,0:T(8,128)(2,1)S(1)}, u32[]{:S(2)}, u32[]{:S(2)}) collective-permute-start(bf16[128,1024]{1,0:T(8,128)(2,1)S(1)} %get-tuple-element.29), channel_id=1, source_target_pairs={{0,6},{2,4},{4,2},{6,0},{1,7},{3,5},{5,3},{7,1},{8,14},{10,12},{12... | collective-permute-start | bytes 786440 | tf_op jit(solution)/shard_map/ppermute | solution.py:51
  97.2 15.7 %all-to-all-done.2 = bf16[8,64,512]{2,1,0:T(8,128)(2,1)S(1)} async-done(((bf16[8,64,512]{2,1,0:T(8,128)(2,1)}), bf16[8,64,512]{2,1,0:T(8,128)(2,1)S(1)}, u32[]{:S(2)}, u32[]{:S(2)}) %all-to-all-start.2) | async-done | bytes 524320 | tf_op jit(solution)/shard_map/all_to_all | solution.py:34
  113.1 11.4 %all_to_all.26.own = bf16[4,2,32,512]{3,2,1,0:T(8,128)(2,1)S(1)} all-to-all(bf16[4,2,32,512]{3,2,1,0:T(8,128)(2,1)S(1)} %broadcast_in_dim.7), channel_id=1, replica_groups=mesh['zh'=4,'zl'=3,'yh'=2,'yl'=4,'x'=4,'c'=2] {'yl'}, dimensions={0} | all-to-all | bytes 524288 | tf_op jit(solution)/shard_map/all_to_all | solution.py:28
  124.6 1.9 %collective-permute-start.9 = (bf16[4,2,32,512]{3,2,1,0:T(8,128)(2,1)S(1)}, bf16[4,2,32,512]{3,2,1,0:T(8,128)(2,1)S(1)}, u32[]{:S(2)}, u32[]{:S(2)}) collective-permute-start(bf16[4,2,32,512]{3,2,1,0:T(8,128)(2,1)S(1)} %all_to_all.26.own), channel_id=1, source_target_pairs={{0,1},{1,0},{2,3},{3,2},{4,5},{5,4},{6,7},{7,6},{8,9},{9,8},{10,11... | collective-permute-start | bytes 786440 | tf_op jit(solution)/shard_map/ppermute | solution.py:19
  126.5 2.4 %collective-permute-start.10 = (f32[2,32,512]{2,1,0:T(8,128)S(1)}, f32[2,32,512]{2,1,0:T(8,128)S(1)}, u32[]{:S(2)}, u32[]{:S(2)}) collective-permute-start(f32[2,32,512]{2,1,0:T(8,128)S(1)} %pad_maximum_fusion.2), channel_id=1, source_target_pairs={{0,1},{1,0},{2,3},{3,2},{4,5},{5,4},{6,7},{7,6},{8,9},{9,8},{10,11... | collective-permute-start | bytes 393224 | tf_op jit(solution)/shard_map/ppermute | solution.py:19
  129.0 2.3 %shard_map.76 = bf16[4,2,128,256]{3,2,1,0:T(8,128)(2,1)} custom-call(s32[2]{0:T(128)S(1)} %pad_add_fusion.place, bf16[4,2,32,512]{3,2,1,0:T(8,128)(2,1)S(1)} %all_to_all.26.own, bf16[4,2,32,512]{3,2,1,0:T(8,128)(2,1)S(1)} %collective-permute-done.9.other, bf16[256,1024]{1,0:T(8,128)(2,1)S(1)} %copy-done.1, ...), custom_call_target="tpu_custom_call" | custom-call | flops 536870912 | bytes 3145728 | tf_op jit(solution)/shard_map/pallas_call | solution.py:85
  131.3 3.5 %all-to-all-start.4 = ((bf16[4,2,128,256]{3,2,1,0:T(8,128)(2,1)}), bf16[4,2,128,256]{3,2,1,0:T(8,128)(2,1)S(1)}, u32[]{:S(2)}, u32[]{:S(2)}) async-start(bf16[4,2,128,256]{3,2,1,0:T(8,128)(2,1)} %shard_map.76), calls=%async_computation.4 | async-start | bytes 1048576 | tf_op jit(solution)/shard_map/all_to_all | solution.py:157
  136.2 8.5 %all-to-all-done.4 = bf16[4,2,128,256]{3,2,1,0:T(8,128)(2,1)S(1)} async-done(((bf16[4,2,128,256]{3,2,1,0:T(8,128)(2,1)}), bf16[4,2,128,256]{3,2,1,0:T(8,128)(2,1)S(1)}, u32[]{:S(2)}, u32[]{:S(2)}) %all-to-all-start.4) | async-done | bytes 524320 | tf_op jit(solution)/shard_map/all_to_all | solution.py:157
  (43 shorter events, 8.4 us)
Async XLA Ops:
  0.6 1.0 copy-start
  0.6 6.0 %copy-start.1 = (bf16[256,1024]{1,0:T(8,128)(2,1)S(1)}, bf16[256,1024]{1,0:T(8,128)(2,1)}, u32[]{:S(2)}) copy-start(bf16[256,1024]{1,0:T(8,128)(2,1)} %refs_0_) | copy-start | bytes 1572868
  2.8 3.8 %collective-permute-start.2 = (bf16[512,512]{1,0:T(8,128)(2,1)S(1)}, bf16[512,512]{1,0:T(8,128)(2,1)S(1)}, u32[]{:S(2)}, u32[]{:S(2)}) collective-permute-start(bf16[512,512]{1,0:T(8,128)(2,1)S(1)} %fusion), channel_id=1, source_target_pairs={{0,1},{1,0},{2,3},{3,2},{4,5},{5,4},{6,7},{7,6},{8,9},{9,8},{10,11... | collective-permute-start | bytes 1572872 | tf_op jit(solution)/shard_map/ppermute | solution.py:19
  31.1 4.4 %copy-start.2 = (bf16[512,24,32]{0,2,1:T(8,128)(2,1)S(1)}, bf16[512,24,32]{0,2,1:T(8,128)(2,1)}, u32[]{:S(2)}) copy-start(bf16[512,24,32]{0,2,1:T(8,128)(2,1)} %param.6) | copy-start | bytes 2359300
  31.9 19.9 %all-to-all-start.1 = ((bf16[16,32,512]{2,1,0:T(8,128)(2,1)}), bf16[16,32,512]{2,1,0:T(8,128)(2,1)S(1)}, u32[]{:S(2)}, u32[]{:S(2)}) async-start(bf16[16,32,512]{2,1,0:T(8,128)(2,1)} %broadcast_in_dim.6), calls=%async_computation.1 | async-start | bytes 1048576 | tf_op jit(solution)/shard_map/all_to_all | solution.py:28
  35.5 4.2 %collective-permute-start.1 = (bf16[24,32,512]{2,1,0:T(8,128)(2,1)S(1)}, bf16[24,32,512]{2,1,0:T(8,128)(2,1)S(1)}, u32[]{:S(2)}, u32[]{:S(2)}) collective-permute-start(bf16[24,32,512]{2,1,0:T(8,128)(2,1)S(1)} %bitcast.80), channel_id=1, source_target_pairs={{0,1},{1,0},{2,3},{3,2},{4,5},{5,4},{6,7},{7,6},{8,9},{9,8},{10,11... | collective-permute-start | bytes 2359304 | tf_op jit(solution)/shard_map/ppermute | solution.py:19
  52.2 14.5 %collective-permute-start.3 = (bf16[512,512]{1,0:T(8,128)(2,1)S(1)}, bf16[512,512]{1,0:T(8,128)(2,1)S(1)}, u32[]{:S(2)}, u32[]{:S(2)}) collective-permute-start(bf16[512,512]{1,0:T(8,128)(2,1)S(1)} %convolution_convert_fusion.1), channel_id=1, source_target_pairs={{0,64},{64,128},{128,192},{192,256},{256,320},{320,384},{384,448},... | collective-permute-start | bytes 1572872 | tf_op jit(solution)/shard_map/ppermute | solution.py:24
  57.0 16.0 %collective-permute-start.4 = (bf16[512,512]{1,0:T(8,128)(2,1)S(1)}, bf16[512,512]{1,0:T(8,128)(2,1)S(1)}, u32[]{:S(2)}, u32[]{:S(2)}) collective-permute-start(bf16[512,512]{1,0:T(8,128)(2,1)S(1)} %convolution_convert_fusion), channel_id=1, source_target_pairs={{0,704},{64,0},{128,64},{192,128},{256,192},{320,256},{384,320},{4... | collective-permute-start | bytes 1572872 | tf_op jit(solution)/shard_map/ppermute | solution.py:24
  58.9 15.3 %collective-permute-start.5 = (bf16[256,1024]{1,0:T(8,128)(2,1)S(1)}, bf16[256,1024]{1,0:T(8,128)(2,1)S(1)}, u32[]{:S(2)}, u32[]{:S(2)}) collective-permute-start(bf16[256,1024]{1,0:T(8,128)(2,1)S(1)} %copy-done.1), channel_id=1, source_target_pairs={{0,2},{2,0},{4,6},{6,4},{1,3},{3,1},{5,7},{7,5},{8,10},{10,8},{12,... | collective-permute-start | bytes 1572872 | tf_op jit(solution)/shard_map/ppermute | solution.py:51
  60.9 13.4 %collective-permute-start.6 = (bf16[128,1024]{1,0:T(8,128)(2,1)S(1)}, bf16[128,1024]{1,0:T(8,128)(2,1)S(1)}, u32[]{:S(2)}, u32[]{:S(2)}) collective-permute-start(bf16[128,1024]{1,0:T(8,128)(2,1)S(1)} %get-tuple-element.30), channel_id=1, source_target_pairs={{0,6},{2,4},{4,2},{6,0},{1,7},{3,5},{5,3},{7,1},{8,14},{10,12},{12... | collective-permute-start | bytes 786440 | tf_op jit(solution)/shard_map/ppermute | solution.py:51
  74.3 14.1 %copy-start.3 = (f32[32,1024]{1,0:T(8,128)S(1)}, f32[32,1024]{1,0:T(8,128)}, u32[]{:S(2)}) copy-start(f32[32,1024]{1,0:T(8,128)} %param.9) | copy-start | bytes 393220
  74.3 14.1 %copy-start.4 = (f32[32,1024]{1,0:T(8,128)S(1)}, f32[32,1024]{1,0:T(8,128)}, u32[]{:S(2)}) copy-start(f32[32,1024]{1,0:T(8,128)} %param.8) | copy-start | bytes 393220
  74.3 38.6 %all-to-all-start.2 = ((bf16[8,64,512]{2,1,0:T(8,128)(2,1)}), bf16[8,64,512]{2,1,0:T(8,128)(2,1)S(1)}, u32[]{:S(2)}, u32[]{:S(2)}) async-start(bf16[8,64,512]{2,1,0:T(8,128)(2,1)} %bitcast.26), calls=%async_computation.2 | async-start | bytes 1048576 | tf_op jit(solution)/shard_map/all_to_all | solution.py:34
  88.4 24.7 %collective-permute-start.7 = (bf16[256,1024]{1,0:T(8,128)(2,1)S(1)}, bf16[256,1024]{1,0:T(8,128)(2,1)S(1)}, u32[]{:S(2)}, u32[]{:S(2)}) collective-permute-start(bf16[256,1024]{1,0:T(8,128)(2,1)S(1)} %copy-done.1), channel_id=1, source_target_pairs={{0,4},{2,6},{4,0},{6,2},{1,5},{3,7},{5,1},{7,3},{8,12},{10,14},{12... | collective-permute-start | bytes 1572872 | tf_op jit(solution)/shard_map/ppermute | solution.py:51
  91.2 21.8 %collective-permute-start = (f32[2,32,512]{2,1,0:T(8,128)S(1)}, f32[2,32,512]{2,1,0:T(8,128)S(1)}, u32[]{:S(2)}, u32[]{:S(2)}) collective-permute-start(f32[2,32,512]{2,1,0:T(8,128)S(1)} %pad_maximum_fusion.1), channel_id=1, source_target_pairs={{0,1},{1,0},{2,3},{3,2},{4,5},{5,4},{6,7},{7,6},{8,9},{9,8},{10,11... | collective-permute-start | bytes 393224 | tf_op jit(solution)/shard_map/ppermute | solution.py:19
  93.2 19.9 %collective-permute-start.8 = (bf16[128,1024]{1,0:T(8,128)(2,1)S(1)}, bf16[128,1024]{1,0:T(8,128)(2,1)S(1)}, u32[]{:S(2)}, u32[]{:S(2)}) collective-permute-start(bf16[128,1024]{1,0:T(8,128)(2,1)S(1)} %get-tuple-element.29), channel_id=1, source_target_pairs={{0,6},{2,4},{4,2},{6,0},{1,7},{3,5},{5,3},{7,1},{8,14},{10,12},{12... | collective-permute-start | bytes 786440 | tf_op jit(solution)/shard_map/ppermute | solution.py:51
  124.6 4.5 %collective-permute-start.9 = (bf16[4,2,32,512]{3,2,1,0:T(8,128)(2,1)S(1)}, bf16[4,2,32,512]{3,2,1,0:T(8,128)(2,1)S(1)}, u32[]{:S(2)}, u32[]{:S(2)}) collective-permute-start(bf16[4,2,32,512]{3,2,1,0:T(8,128)(2,1)S(1)} %all_to_all.26.own), channel_id=1, source_target_pairs={{0,1},{1,0},{2,3},{3,2},{4,5},{5,4},{6,7},{7,6},{8,9},{9,8},{10,11... | collective-permute-start | bytes 786440 | tf_op jit(solution)/shard_map/ppermute | solution.py:19
  126.5 8.2 %collective-permute-start.10 = (f32[2,32,512]{2,1,0:T(8,128)S(1)}, f32[2,32,512]{2,1,0:T(8,128)S(1)}, u32[]{:S(2)}, u32[]{:S(2)}) collective-permute-start(f32[2,32,512]{2,1,0:T(8,128)S(1)} %pad_maximum_fusion.2), channel_id=1, source_target_pairs={{0,1},{1,0},{2,3},{3,2},{4,5},{5,4},{6,7},{7,6},{8,9},{9,8},{10,11... | collective-permute-start | bytes 393224 | tf_op jit(solution)/shard_map/ppermute | solution.py:19
  131.3 13.4 %all-to-all-start.4 = ((bf16[4,2,128,256]{3,2,1,0:T(8,128)(2,1)}), bf16[4,2,128,256]{3,2,1,0:T(8,128)(2,1)S(1)}, u32[]{:S(2)}, u32[]{:S(2)}) async-start(bf16[4,2,128,256]{3,2,1,0:T(8,128)(2,1)} %shard_map.76), calls=%async_computation.4 | async-start | bytes 1048576 | tf_op jit(solution)/shard_map/all_to_all | solution.py:157

commit v6 on v5

--- a/solution.py
+++ b/solution.py
@@ -116,7 +116,7 @@
 
     late, projected = lax.optimization_barrier((basis, projected))
     near = [[late]] + [[across(late, "x", n_x, flip)] for flip in range(1, n_x - 1)]
-    near.append([across(part, "x", n_x, n_x - 1) for part in jnp.split(late, 2)])
+    near.append([across(part, "x", n_x, n_x - 1) for part in jnp.split(late, [3 * late.shape[0] // 4])])
 
     both = jnp.stack([mine, theirs]).reshape(n_c, n_zh, n_zl, n_yh, cols, tokens)
 

time: 146 us -> 147 us (level)
  transfers between devices with their start and end apart: 14 -> 14, of which waited for: 7 -> 7; matrix products, arithmetic and copies ran while one was open for 3% -> 2% of each run, Pallas kernels for 2% -> 2%
where the time goes in v6:
time: 147 us; the launch traced here: 146 us
  starting transfers between devices  50 us (34%)
  waiting for transfers between devices  49 us (33%)
  blocking collectives  35.4 us (24%)
  matrix products  3.66 us (2%)
  local copies, waits for them, and re-layouts  2.83 us (2%)
  Pallas kernels  2.32 us (2%)
  other arithmetic  1.85 us (1%)
    all_to_all x1, blocking collectives, scatter_sum(): parts = lax.all_to_all(parts, axes, 0, 0).astype(F32)  24 us
    all_to_all x1, waiting for transfers between devices, scatter_sum(): parts = lax.all_to_all(parts, axes, 0, 0).astype(F32)  15.7 us
    all_to_all x1, starting transfers between devices, scatter_sum(): parts = lax.all_to_all(parts, axes, 0, 0).astype(F32)  14.4 us
    ppermute x4, starting transfers between devices, across(): return lax.ppermute(array, axis, [(i, i ^ flip) for i in range(count)])  12.2 us
    all_to_all x1, waiting for transfers between devices, gather(): lax.all_to_all(jnp.broadcast_to(array, (count,) + array.shape), axes, 0, 0)  11.9 us
    all_to_all x1, blocking collectives, gather(): lax.all_to_all(jnp.broadcast_to(array, (count,) + array.shape), axes, 0, 0)  11.3 us
    ppermute x5, starting transfers between devices, swap(): return lax.ppermute(array, axis, [(0, 1), (1, 0)])  10.1 us
    ppermute x2, waiting for transfers between devices, along_z(): lax.ppermute(array, ('zh', 'zl'), [(i, (i + step) % count) for i in range...  8.78 us
  transfers between devices with their start and end apart: 14, of which 7 were waited for; matrix products, arithmetic and copies ran while one was open for 2% of the time, Pallas kernels for 2%

profile of v6, /device:TPU:128, one launch (start us, length us, event | category | flops | bytes accessed | tf_op | source)
XLA Modules:
  0.0 146.1 jit_solution(4917507682627648407)
XLA Ops:
  2.8 1.9 %collective-permute-start.2 = (bf16[512,512]{1,0:T(8,128)(2,1)S(1)}, bf16[512,512]{1,0:T(8,128)(2,1)S(1)}, u32[]{:S(2)}, u32[]{:S(2)}) collective-permute-start(bf16[512,512]{1,0:T(8,128)(2,1)S(1)} %fusion), channel_id=1, source_target_pairs={{0,1},{1,0},{2,3},{3,2},{4,5},{5,4},{6,7},{7,6},{8,9},{9,8},{10,11... | collective-permute-start | bytes 1572872 | tf_op jit(solution)/shard_map/ppermute | solution.py:19
  4.8 1.9 %collective-permute-done.2 = bf16[512,512]{1,0:T(8,128)(2,1)S(1)} collective-permute-done((bf16[512,512]{1,0:T(8,128)(2,1)S(1)}, bf16[512,512]{1,0:T(8,128)(2,1)S(1)}, u32[]{:S(2)}, u32[]{:S(2)}) %collective-permute-start.2) | collective-permute-done | bytes 524320 | tf_op jit(solution)/shard_map/ppermute | solution.py:19
  6.9 24.0 %all_to_all.25 = bf16[16,32,512]{2,1,0:T(8,128)(2,1)S(1)} all-to-all(bf16[16,32,512]{2,1,0:T(8,128)(2,1)S(1)} %bitcast.79), channel_id=1, replica_groups=mesh['zh'=4,'zl'=3,'yh'=2,'yl'=4,'x'=4,'c'=2] {'x','yl'}, dimensions={0} | all-to-all | bytes 1048576 | tf_op jit(solution)/shard_map/all_to_all | solution.py:34
  31.9 3.6 %all-to-all-start.1 = ((bf16[16,32,512]{2,1,0:T(8,128)(2,1)}), bf16[16,32,512]{2,1,0:T(8,128)(2,1)S(1)}, u32[]{:S(2)}, u32[]{:S(2)}) async-start(bf16[16,32,512]{2,1,0:T(8,128)(2,1)} %broadcast_in_dim.6), calls=%async_computation.1 | async-start | bytes 1048576 | tf_op jit(solution)/shard_map/all_to_all | solution.py:28
  35.5 1.9 %collective-permute-start.1 = (bf16[24,32,512]{2,1,0:T(8,128)(2,1)S(1)}, bf16[24,32,512]{2,1,0:T(8,128)(2,1)S(1)}, u32[]{:S(2)}, u32[]{:S(2)}) collective-permute-start(bf16[24,32,512]{2,1,0:T(8,128)(2,1)S(1)} %bitcast.80), channel_id=1, source_target_pairs={{0,1},{1,0},{2,3},{3,2},{4,5},{5,4},{6,7},{7,6},{8,9},{9,8},{10,11... | collective-permute-start | bytes 2359304 | tf_op jit(solution)/shard_map/ppermute | solution.py:19
  37.5 2.2 %collective-permute-done.1 = bf16[24,32,512]{2,1,0:T(8,128)(2,1)S(1)} collective-permute-done((bf16[24,32,512]{2,1,0:T(8,128)(2,1)S(1)}, bf16[24,32,512]{2,1,0:T(8,128)(2,1)S(1)}, u32[]{:S(2)}, u32[]{:S(2)}) %collective-permute-start.1) | collective-permute-done | bytes 786464 | tf_op jit(solution)/shard_map/ppermute | solution.py:19
  39.9 11.9 %all-to-all-done.1 = bf16[16,32,512]{2,1,0:T(8,128)(2,1)S(1)} async-done(((bf16[16,32,512]{2,1,0:T(8,128)(2,1)}), bf16[16,32,512]{2,1,0:T(8,128)(2,1)S(1)}, u32[]{:S(2)}, u32[]{:S(2)}) %all-to-all-start.1) | async-done | bytes 524320 | tf_op jit(solution)/shard_map/all_to_all | solution.py:28
  52.2 4.3 %collective-permute-start.3 = (bf16[512,512]{1,0:T(8,128)(2,1)S(1)}, bf16[512,512]{1,0:T(8,128)(2,1)S(1)}, u32[]{:S(2)}, u32[]{:S(2)}) collective-permute-start(bf16[512,512]{1,0:T(8,128)(2,1)S(1)} %convolution_convert_fusion.1), channel_id=1, source_target_pairs={{0,64},{64,128},{128,192},{192,256},{256,320},{320,384},{384,448},... | collective-permute-start | bytes 1572872 | tf_op jit(solution)/shard_map/ppermute | solution.py:24
  57.0 1.9 %collective-permute-start.4 = (bf16[512,512]{1,0:T(8,128)(2,1)S(1)}, bf16[512,512]{1,0:T(8,128)(2,1)S(1)}, u32[]{:S(2)}, u32[]{:S(2)}) collective-permute-start(bf16[512,512]{1,0:T(8,128)(2,1)S(1)} %convolution_convert_fusion), channel_id=1, source_target_pairs={{0,704},{64,0},{128,64},{192,128},{256,192},{320,256},{384,320},{4... | collective-permute-start | bytes 1572872 | tf_op jit(solution)/shard_map/ppermute | solution.py:24
  58.9 1.9 %collective-permute-start.5 = (bf16[256,1024]{1,0:T(8,128)(2,1)S(1)}, bf16[256,1024]{1,0:T(8,128)(2,1)S(1)}, u32[]{:S(2)}, u32[]{:S(2)}) collective-permute-start(bf16[256,1024]{1,0:T(8,128)(2,1)S(1)} %copy-done.1), channel_id=1, source_target_pairs={{0,2},{2,0},{4,6},{6,4},{1,3},{3,1},{5,7},{7,5},{8,10},{10,8},{12,... | collective-permute-start | bytes 1572872 | tf_op jit(solution)/shard_map/ppermute | solution.py:51
  60.9 3.3 %collective-permute-start.6 = (bf16[192,1024]{1,0:T(8,128)(2,1)S(1)}, bf16[192,1024]{1,0:T(8,128)(2,1)S(1)}, u32[]{:S(2)}, u32[]{:S(2)}) collective-permute-start(bf16[192,1024]{1,0:T(8,128)(2,1)S(1)} %split.6), channel_id=1, source_target_pairs={{0,6},{2,4},{4,2},{6,0},{1,7},{3,5},{5,3},{7,1},{8,14},{10,12},{12... | collective-permute-start | bytes 1179656 | tf_op jit(solution)/shard_map/ppermute | solution.py:51
  64.2 2.5 %collective-permute-done.3 = bf16[512,512]{1,0:T(8,128)(2,1)S(1)} collective-permute-done((bf16[512,512]{1,0:T(8,128)(2,1)S(1)}, bf16[512,512]{1,0:T(8,128)(2,1)S(1)}, u32[]{:S(2)}, u32[]{:S(2)}) %collective-permute-start.3) | collective-permute-done | bytes 524320 | tf_op jit(solution)/shard_map/ppermute | solution.py:24
  66.7 6.3 %collective-permute-done.4 = bf16[512,512]{1,0:T(8,128)(2,1)S(1)} collective-permute-done((bf16[512,512]{1,0:T(8,128)(2,1)S(1)}, bf16[512,512]{1,0:T(8,128)(2,1)S(1)}, u32[]{:S(2)}, u32[]{:S(2)}) %collective-permute-start.4) | collective-permute-done | bytes 524320 | tf_op jit(solution)/shard_map/ppermute | solution.py:24
  74.3 14.4 %all-to-all-start.2 = ((bf16[8,64,512]{2,1,0:T(8,128)(2,1)}), bf16[8,64,512]{2,1,0:T(8,128)(2,1)S(1)}, u32[]{:S(2)}, u32[]{:S(2)}) async-start(bf16[8,64,512]{2,1,0:T(8,128)(2,1)} %bitcast.26), calls=%async_computation.2 | async-start | bytes 1048576 | tf_op jit(solution)/shard_map/all_to_all | solution.py:34
  88.8 2.8 %collective-permute-start.7 = (bf16[256,1024]{1,0:T(8,128)(2,1)S(1)}, bf16[256,1024]{1,0:T(8,128)(2,1)S(1)}, u32[]{:S(2)}, u32[]{:S(2)}) collective-permute-start(bf16[256,1024]{1,0:T(8,128)(2,1)S(1)} %copy-done.1), channel_id=1, source_target_pairs={{0,4},{2,6},{4,0},{6,2},{1,5},{3,7},{5,1},{7,3},{8,12},{10,14},{12... | collective-permute-start | bytes 1572872 | tf_op jit(solution)/shard_map/ppermute | solution.py:51
  91.5 1.9 %collective-permute-start = (f32[2,32,512]{2,1,0:T(8,128)S(1)}, f32[2,32,512]{2,1,0:T(8,128)S(1)}, u32[]{:S(2)}, u32[]{:S(2)}) collective-permute-start(f32[2,32,512]{2,1,0:T(8,128)S(1)} %pad_maximum_fusion.1), channel_id=1, source_target_pairs={{0,1},{1,0},{2,3},{3,2},{4,5},{5,4},{6,7},{7,6},{8,9},{9,8},{10,11... | collective-permute-start | bytes 393224 | tf_op jit(solution)/shard_map/ppermute | solution.py:19
  93.5 4.2 %collective-permute-start.8 = (bf16[64,1024]{1,0:T(8,128)(2,1)S(1)}, bf16[64,1024]{1,0:T(8,128)(2,1)S(1)}, u32[]{:S(2)}, u32[]{:S(2)}) collective-permute-start(bf16[64,1024]{1,0:T(8,128)(2,1)S(1)} %split.7), channel_id=1, source_target_pairs={{0,6},{2,4},{4,2},{6,0},{1,7},{3,5},{5,3},{7,1},{8,14},{10,12},{12... | collective-permute-start | bytes 393224 | tf_op jit(solution)/shard_map/ppermute | solution.py:51
  97.8 15.7 %all-to-all-done.2 = bf16[8,64,512]{2,1,0:T(8,128)(2,1)S(1)} async-done(((bf16[8,64,512]{2,1,0:T(8,128)(2,1)}), bf16[8,64,512]{2,1,0:T(8,128)(2,1)S(1)}, u32[]{:S(2)}, u32[]{:S(2)}) %all-to-all-start.2) | async-done | bytes 524320 | tf_op jit(solution)/shard_map/all_to_all | solution.py:34
  113.7 11.3 %all_to_all.26.own = bf16[4,2,32,512]{3,2,1,0:T(8,128)(2,1)S(1)} all-to-all(bf16[4,2,32,512]{3,2,1,0:T(8,128)(2,1)S(1)} %broadcast_in_dim.7), channel_id=1, replica_groups=mesh['zh'=4,'zl'=3,'yh'=2,'yl'=4,'x'=4,'c'=2] {'yl'}, dimensions={0} | all-to-all | bytes 524288 | tf_op jit(solution)/shard_map/all_to_all | solution.py:28
  125.1 1.9 %collective-permute-start.9 = (bf16[4,2,32,512]{3,2,1,0:T(8,128)(2,1)S(1)}, bf16[4,2,32,512]{3,2,1,0:T(8,128)(2,1)S(1)}, u32[]{:S(2)}, u32[]{:S(2)}) collective-permute-start(bf16[4,2,32,512]{3,2,1,0:T(8,128)(2,1)S(1)} %all_to_all.26.own), channel_id=1, source_target_pairs={{0,1},{1,0},{2,3},{3,2},{4,5},{5,4},{6,7},{7,6},{8,9},{9,8},{10,11... | collective-permute-start | bytes 786440 | tf_op jit(solution)/shard_map/ppermute | solution.py:19
  127.1 2.4 %collective-permute-start.10 = (f32[2,32,512]{2,1,0:T(8,128)S(1)}, f32[2,32,512]{2,1,0:T(8,128)S(1)}, u32[]{:S(2)}, u32[]{:S(2)}) collective-permute-start(f32[2,32,512]{2,1,0:T(8,128)S(1)} %pad_maximum_fusion.2), channel_id=1, source_target_pairs={{0,1},{1,0},{2,3},{3,2},{4,5},{5,4},{6,7},{7,6},{8,9},{9,8},{10,11... | collective-permute-start | bytes 393224 | tf_op jit(solution)/shard_map/ppermute | solution.py:19
  129.5 2.3 %shard_map.76 = bf16[4,2,128,256]{3,2,1,0:T(8,128)(2,1)} custom-call(s32[2]{0:T(128)S(1)} %pad_add_fusion.place, bf16[4,2,32,512]{3,2,1,0:T(8,128)(2,1)S(1)} %all_to_all.26.own, bf16[4,2,32,512]{3,2,1,0:T(8,128)(2,1)S(1)} %collective-permute-done.9.other, bf16[256,1024]{1,0:T(8,128)(2,1)S(1)} %copy-done.1, ...), custom_call_target="tpu_custom_call" | custom-call | flops 536870912 | bytes 3145728 | tf_op jit(solution)/shard_map/pallas_call | solution.py:85
  131.9 3.5 %all-to-all-start.4 = ((bf16[4,2,128,256]{3,2,1,0:T(8,128)(2,1)}), bf16[4,2,128,256]{3,2,1,0:T(8,128)(2,1)S(1)}, u32[]{:S(2)}, u32[]{:S(2)}) async-start(bf16[4,2,128,256]{3,2,1,0:T(8,128)(2,1)} %shard_map.76), calls=%async_computation.4 | async-start | bytes 1048576 | tf_op jit(solution)/shard_map/all_to_all | solution.py:157
  136.7 8.5 %all-to-all-done.4 = bf16[4,2,128,256]{3,2,1,0:T(8,128)(2,1)S(1)} async-done(((bf16[4,2,128,256]{3,2,1,0:T(8,128)(2,1)}), bf16[4,2,128,256]{3,2,1,0:T(8,128)(2,1)S(1)}, u32[]{:S(2)}, u32[]{:S(2)}) %all-to-all-start.4) | async-done | bytes 524320 | tf_op jit(solution)/shard_map/all_to_all | solution.py:157
  (44 shorter events, 8.4 us)
Async XLA Ops:
  0.6 1.0 copy-start
  0.6 6.0 %copy-start.1 = (bf16[256,1024]{1,0:T(8,128)(2,1)S(1)}, bf16[256,1024]{1,0:T(8,128)(2,1)}, u32[]{:S(2)}) copy-start(bf16[256,1024]{1,0:T(8,128)(2,1)} %refs_0_) | copy-start | bytes 1572868
  2.8 3.8 %collective-permute-start.2 = (bf16[512,512]{1,0:T(8,128)(2,1)S(1)}, bf16[512,512]{1,0:T(8,128)(2,1)S(1)}, u32[]{:S(2)}, u32[]{:S(2)}) collective-permute-start(bf16[512,512]{1,0:T(8,128)(2,1)S(1)} %fusion), channel_id=1, source_target_pairs={{0,1},{1,0},{2,3},{3,2},{4,5},{5,4},{6,7},{7,6},{8,9},{9,8},{10,11... | collective-permute-start | bytes 1572872 | tf_op jit(solution)/shard_map/ppermute | solution.py:19
  31.1 4.4 %copy-start.2 = (bf16[512,24,32]{0,2,1:T(8,128)(2,1)S(1)}, bf16[512,24,32]{0,2,1:T(8,128)(2,1)}, u32[]{:S(2)}) copy-start(bf16[512,24,32]{0,2,1:T(8,128)(2,1)} %param.6) | copy-start | bytes 2359300
  31.9 19.9 %all-to-all-start.1 = ((bf16[16,32,512]{2,1,0:T(8,128)(2,1)}), bf16[16,32,512]{2,1,0:T(8,128)(2,1)S(1)}, u32[]{:S(2)}, u32[]{:S(2)}) async-start(bf16[16,32,512]{2,1,0:T(8,128)(2,1)} %broadcast_in_dim.6), calls=%async_computation.1 | async-start | bytes 1048576 | tf_op jit(solution)/shard_map/all_to_all | solution.py:28
  35.5 4.2 %collective-permute-start.1 = (bf16[24,32,512]{2,1,0:T(8,128)(2,1)S(1)}, bf16[24,32,512]{2,1,0:T(8,128)(2,1)S(1)}, u32[]{:S(2)}, u32[]{:S(2)}) collective-permute-start(bf16[24,32,512]{2,1,0:T(8,128)(2,1)S(1)} %bitcast.80), channel_id=1, source_target_pairs={{0,1},{1,0},{2,3},{3,2},{4,5},{5,4},{6,7},{7,6},{8,9},{9,8},{10,11... | collective-permute-start | bytes 2359304 | tf_op jit(solution)/shard_map/ppermute | solution.py:19
  52.2 14.5 %collective-permute-start.3 = (bf16[512,512]{1,0:T(8,128)(2,1)S(1)}, bf16[512,512]{1,0:T(8,128)(2,1)S(1)}, u32[]{:S(2)}, u32[]{:S(2)}) collective-permute-start(bf16[512,512]{1,0:T(8,128)(2,1)S(1)} %convolution_convert_fusion.1), channel_id=1, source_target_pairs={{0,64},{64,128},{128,192},{192,256},{256,320},{320,384},{384,448},... | collective-permute-start | bytes 1572872 | tf_op jit(solution)/shard_map/ppermute | solution.py:24
  57.0 16.0 %collective-permute-start.4 = (bf16[512,512]{1,0:T(8,128)(2,1)S(1)}, bf16[512,512]{1,0:T(8,128)(2,1)S(1)}, u32[]{:S(2)}, u32[]{:S(2)}) collective-permute-start(bf16[512,512]{1,0:T(8,128)(2,1)S(1)} %convolution_convert_fusion), channel_id=1, source_target_pairs={{0,704},{64,0},{128,64},{192,128},{256,192},{320,256},{384,320},{4... | collective-permute-start | bytes 1572872 | tf_op jit(solution)/shard_map/ppermute | solution.py:24
  58.9 15.4 %collective-permute-start.5 = (bf16[256,1024]{1,0:T(8,128)(2,1)S(1)}, bf16[256,1024]{1,0:T(8,128)(2,1)S(1)}, u32[]{:S(2)}, u32[]{:S(2)}) collective-permute-start(bf16[256,1024]{1,0:T(8,128)(2,1)S(1)} %copy-done.1), channel_id=1, source_target_pairs={{0,2},{2,0},{4,6},{6,4},{1,3},{3,1},{5,7},{7,5},{8,10},{10,8},{12,... | collective-permute-start | bytes 1572872 | tf_op jit(solution)/shard_map/ppermute | solution.py:51
  60.9 13.4 %collective-permute-start.6 = (bf16[192,1024]{1,0:T(8,128)(2,1)S(1)}, bf16[192,1024]{1,0:T(8,128)(2,1)S(1)}, u32[]{:S(2)}, u32[]{:S(2)}) collective-permute-start(bf16[192,1024]{1,0:T(8,128)(2,1)S(1)} %split.6), channel_id=1, source_target_pairs={{0,6},{2,4},{4,2},{6,0},{1,7},{3,5},{5,3},{7,1},{8,14},{10,12},{12... | collective-permute-start | bytes 1179656 | tf_op jit(solution)/shard_map/ppermute | solution.py:51
  74.3 14.4 %copy-start.3 = (f32[32,1024]{1,0:T(8,128)S(1)}, f32[32,1024]{1,0:T(8,128)}, u32[]{:S(2)}) copy-start(f32[32,1024]{1,0:T(8,128)} %param.9) | copy-start | bytes 393220
  74.3 14.4 %copy-start.4 = (f32[32,1024]{1,0:T(8,128)S(1)}, f32[32,1024]{1,0:T(8,128)}, u32[]{:S(2)}) copy-start(f32[32,1024]{1,0:T(8,128)} %param.8) | copy-start | bytes 393220
  74.3 39.2 %all-to-all-start.2 = ((bf16[8,64,512]{2,1,0:T(8,128)(2,1)}), bf16[8,64,512]{2,1,0:T(8,128)(2,1)S(1)}, u32[]{:S(2)}, u32[]{:S(2)}) async-start(bf16[8,64,512]{2,1,0:T(8,128)(2,1)} %bitcast.26), calls=%async_computation.2 | async-start | bytes 1048576 | tf_op jit(solution)/shard_map/all_to_all | solution.py:34
  88.8 24.9 %collective-permute-start.7 = (bf16[256,1024]{1,0:T(8,128)(2,1)S(1)}, bf16[256,1024]{1,0:T(8,128)(2,1)S(1)}, u32[]{:S(2)}, u32[]{:S(2)}) collective-permute-start(bf16[256,1024]{1,0:T(8,128)(2,1)S(1)} %copy-done.1), channel_id=1, source_target_pairs={{0,4},{2,6},{4,0},{6,2},{1,5},{3,7},{5,1},{7,3},{8,12},{10,14},{12... | collective-permute-start | bytes 1572872 | tf_op jit(solution)/shard_map/ppermute | solution.py:51
  91.5 22.0 %collective-permute-start = (f32[2,32,512]{2,1,0:T(8,128)S(1)}, f32[2,32,512]{2,1,0:T(8,128)S(1)}, u32[]{:S(2)}, u32[]{:S(2)}) collective-permute-start(f32[2,32,512]{2,1,0:T(8,128)S(1)} %pad_maximum_fusion.1), channel_id=1, source_target_pairs={{0,1},{1,0},{2,3},{3,2},{4,5},{5,4},{6,7},{7,6},{8,9},{9,8},{10,11... | collective-permute-start | bytes 393224 | tf_op jit(solution)/shard_map/ppermute | solution.py:19
  93.5 20.2 %collective-permute-start.8 = (bf16[64,1024]{1,0:T(8,128)(2,1)S(1)}, bf16[64,1024]{1,0:T(8,128)(2,1)S(1)}, u32[]{:S(2)}, u32[]{:S(2)}) collective-permute-start(bf16[64,1024]{1,0:T(8,128)(2,1)S(1)} %split.7), channel_id=1, source_target_pairs={{0,6},{2,4},{4,2},{6,0},{1,7},{3,5},{5,3},{7,1},{8,14},{10,12},{12... | collective-permute-start | bytes 393224 | tf_op jit(solution)/shard_map/ppermute | solution.py:51
  125.1 4.5 %collective-permute-start.9 = (bf16[4,2,32,512]{3,2,1,0:T(8,128)(2,1)S(1)}, bf16[4,2,32,512]{3,2,1,0:T(8,128)(2,1)S(1)}, u32[]{:S(2)}, u32[]{:S(2)}) collective-permute-start(bf16[4,2,32,512]{3,2,1,0:T(8,128)(2,1)S(1)} %all_to_all.26.own), channel_id=1, source_target_pairs={{0,1},{1,0},{2,3},{3,2},{4,5},{5,4},{6,7},{7,6},{8,9},{9,8},{10,11... | collective-permute-start | bytes 786440 | tf_op jit(solution)/shard_map/ppermute | solution.py:19
  127.1 8.3 %collective-permute-start.10 = (f32[2,32,512]{2,1,0:T(8,128)S(1)}, f32[2,32,512]{2,1,0:T(8,128)S(1)}, u32[]{:S(2)}, u32[]{:S(2)}) collective-permute-start(f32[2,32,512]{2,1,0:T(8,128)S(1)} %pad_maximum_fusion.2), channel_id=1, source_target_pairs={{0,1},{1,0},{2,3},{3,2},{4,5},{5,4},{6,7},{7,6},{8,9},{9,8},{10,11... | collective-permute-start | bytes 393224 | tf_op jit(solution)/shard_map/ppermute | solution.py:19
  131.9 13.4 %all-to-all-start.4 = ((bf16[4,2,128,256]{3,2,1,0:T(8,128)(2,1)}), bf16[4,2,128,256]{3,2,1,0:T(8,128)(2,1)S(1)}, u32[]{:S(2)}, u32[]{:S(2)}) async-start(bf16[4,2,128,256]{3,2,1,0:T(8,128)(2,1)} %shard_map.76), calls=%async_computation.4 | async-start | bytes 1048576 | tf_op jit(solution)/shard_map/all_to_all | solution.py:157

commit v7 on v6

--- a/solution.py
+++ b/solution.py
@@ -147,6 +147,7 @@
 
     rows = gather(direction, "yl", n_yl)
     back = swap(jnp.stack([moment_new[1], second_new[1]]), "c")
+    rows, back = lax.optimization_barrier((rows, back))
 
     def whole(own, other):
         return jnp.concatenate(

time: 147 us -> 148 us (level)
  blocking collectives: 35.4 us -> 24 us
  waiting for transfers between devices: 49 us -> 57.5 us
  starting transfers between devices: 50 us -> 52.9 us
    all_to_all x1 -> x0, blocking collectives: 11.3 us -> none  [gather(): lax.all_to_all(jnp.broadcast_to(array, (count,) + array.shape), axes, 0, 0)]
    all_to_all x1 -> x2, waiting for transfers between devices: 11.9 us -> 17.5 us  [gather(): lax.all_to_all(jnp.broadcast_to(array, (count,) + array.shape), axes, 0, 0)]
    all_to_all x1 -> x2, starting transfers between devices: 3.57 us -> 6.98 us  [gather(): lax.all_to_all(jnp.broadcast_to(array, (count,) + array.shape), axes, 0, 0)]
    ppermute x5, waiting for transfers between devices: 4.07 us -> 6.79 us  [swap(): return lax.ppermute(array, axis, [(0, 1), (1, 0)])]
  transfers between devices with their start and end apart: 14 -> 15, of which waited for: 7 -> 10; matrix products, arithmetic and copies ran while one was open for 2% -> 2% of each run, Pallas kernels for 2% -> 0%
where the time goes in v7:
time: 148 us; the launch traced here: 147 us
  waiting for transfers between devices  57.5 us (39%)
  starting transfers between devices  52.9 us (36%)
  blocking collectives  24 us (16%)
  matrix products  3.66 us (2%)
  local copies, waits for them, and re-layouts  3.54 us (2%)
  Pallas kernels  2.32 us (2%)
  other arithmetic  1.85 us (1%)
    all_to_all x1, blocking collectives, scatter_sum(): parts = lax.all_to_all(parts, axes, 0, 0).astype(F32)  24 us
    all_to_all x2, waiting for transfers between devices, gather(): lax.all_to_all(jnp.broadcast_to(array, (count,) + array.shape), axes, 0, 0)  17.5 us
    all_to_all x1, waiting for transfers between devices, scatter_sum(): parts = lax.all_to_all(parts, axes, 0, 0).astype(F32)  15.7 us
    all_to_all x1, starting transfers between devices, scatter_sum(): parts = lax.all_to_all(parts, axes, 0, 0).astype(F32)  14.4 us
    ppermute x4, starting transfers between devices, across(): return lax.ppermute(array, axis, [(i, i ^ flip) for i in range(count)])  12.2 us
    ppermute x5, starting transfers between devices, swap(): return lax.ppermute(array, axis, [(0, 1), (1, 0)])  9.59 us
    ppermute x2, waiting for transfers between devices, along_z(): lax.ppermute(array, ('zh', 'zl'), [(i, (i + step) % count) for i in range...  8.78 us
    all_to_all x1, waiting for transfers between devices, per_device(): update = lax.all_to_all(update, 'x', 0, 0)  8.66 us
  transfers between devices with their start and end apart: 15, of which 10 were waited for; matrix products, arithmetic and copies ran while one was open for 2% of the time, Pallas kernels for 0%

profile of v7, /device:TPU:128, one launch (start us, length us, event | category | flops | bytes accessed | tf_op | source)
XLA Modules:
  0.0 146.9 jit_solution(16101972281778066023)
XLA Ops:
  2.8 1.9 %collective-permute-start.2 = (bf16[512,512]{1,0:T(8,128)(2,1)S(1)}, bf16[512,512]{1,0:T(8,128)(2,1)S(1)}, u32[]{:S(2)}, u32[]{:S(2)}) collective-permute-start(bf16[512,512]{1,0:T(8,128)(2,1)S(1)} %fusion), channel_id=1, source_target_pairs={{0,1},{1,0},{2,3},{3,2},{4,5},{5,4},{6,7},{7,6},{8,9},{9,8},{10,11... | collective-permute-start | bytes 1572872 | tf_op jit(solution)/shard_map/ppermute | solution.py:19
  6.9 24.0 %all_to_all.25 = bf16[16,32,512]{2,1,0:T(8,128)(2,1)S(1)} all-to-all(bf16[16,32,512]{2,1,0:T(8,128)(2,1)S(1)} %bitcast.79), channel_id=1, replica_groups=mesh['zh'=4,'zl'=3,'yh'=2,'yl'=4,'x'=4,'c'=2] {'x','yl'}, dimensions={0} | all-to-all | bytes 1048576 | tf_op jit(solution)/shard_map/all_to_all | solution.py:34
  31.9 3.6 %all-to-all-start.1 = ((bf16[16,32,512]{2,1,0:T(8,128)(2,1)}), bf16[16,32,512]{2,1,0:T(8,128)(2,1)S(1)}, u32[]{:S(2)}, u32[]{:S(2)}) async-start(bf16[16,32,512]{2,1,0:T(8,128)(2,1)} %broadcast_in_dim.6), calls=%async_computation.1 | async-start | bytes 1048576 | tf_op jit(solution)/shard_map/all_to_all | solution.py:28
  35.5 1.9 %collective-permute-start.1 = (bf16[24,32,512]{2,1,0:T(8,128)(2,1)S(1)}, bf16[24,32,512]{2,1,0:T(8,128)(2,1)S(1)}, u32[]{:S(2)}, u32[]{:S(2)}) collective-permute-start(bf16[24,32,512]{2,1,0:T(8,128)(2,1)S(1)} %bitcast.80), channel_id=1, source_target_pairs={{0,1},{1,0},{2,3},{3,2},{4,5},{5,4},{6,7},{7,6},{8,9},{9,8},{10,11... | collective-permute-start | bytes 2359304 | tf_op jit(solution)/shard_map/ppermute | solution.py:19
  37.5 2.2 %collective-permute-done.1 = bf16[24,32,512]{2,1,0:T(8,128)(2,1)S(1)} collective-permute-done((bf16[24,32,512]{2,1,0:T(8,128)(2,1)S(1)}, bf16[24,32,512]{2,1,0:T(8,128)(2,1)S(1)}, u32[]{:S(2)}, u32[]{:S(2)}) %collective-permute-start.1) | collective-permute-done | bytes 786464 | tf_op jit(solution)/shard_map/ppermute | solution.py:19
  39.9 11.9 %all-to-all-done.1 = bf16[16,32,512]{2,1,0:T(8,128)(2,1)S(1)} async-done(((bf16[16,32,512]{2,1,0:T(8,128)(2,1)}), bf16[16,32,512]{2,1,0:T(8,128)(2,1)S(1)}, u32[]{:S(2)}, u32[]{:S(2)}) %all-to-all-start.1) | async-done | bytes 524320 | tf_op jit(solution)/shard_map/all_to_all | solution.py:28
  52.2 4.3 %collective-permute-start.3 = (bf16[512,512]{1,0:T(8,128)(2,1)S(1)}, bf16[512,512]{1,0:T(8,128)(2,1)S(1)}, u32[]{:S(2)}, u32[]{:S(2)}) collective-permute-start(bf16[512,512]{1,0:T(8,128)(2,1)S(1)} %convolution_convert_fusion.1), channel_id=1, source_target_pairs={{0,64},{64,128},{128,192},{192,256},{256,320},{320,384},{384,448},... | collective-permute-start | bytes 1572872 | tf_op jit(solution)/shard_map/ppermute | solution.py:24
  57.0 1.9 %collective-permute-start.4 = (bf16[512,512]{1,0:T(8,128)(2,1)S(1)}, bf16[512,512]{1,0:T(8,128)(2,1)S(1)}, u32[]{:S(2)}, u32[]{:S(2)}) collective-permute-start(bf16[512,512]{1,0:T(8,128)(2,1)S(1)} %convolution_convert_fusion), channel_id=1, source_target_pairs={{0,704},{64,0},{128,64},{192,128},{256,192},{320,256},{384,320},{4... | collective-permute-start | bytes 1572872 | tf_op jit(solution)/shard_map/ppermute | solution.py:24
  58.9 1.9 %collective-permute-start.5 = (bf16[256,1024]{1,0:T(8,128)(2,1)S(1)}, bf16[256,1024]{1,0:T(8,128)(2,1)S(1)}, u32[]{:S(2)}, u32[]{:S(2)}) collective-permute-start(bf16[256,1024]{1,0:T(8,128)(2,1)S(1)} %copy-done.1), channel_id=1, source_target_pairs={{0,2},{2,0},{4,6},{6,4},{1,3},{3,1},{5,7},{7,5},{8,10},{10,8},{12,... | collective-permute-start | bytes 1572872 | tf_op jit(solution)/shard_map/ppermute | solution.py:51
  60.9 3.3 %collective-permute-start.6 = (bf16[192,1024]{1,0:T(8,128)(2,1)S(1)}, bf16[192,1024]{1,0:T(8,128)(2,1)S(1)}, u32[]{:S(2)}, u32[]{:S(2)}) collective-permute-start(bf16[192,1024]{1,0:T(8,128)(2,1)S(1)} %split.6), channel_id=1, source_target_pairs={{0,6},{2,4},{4,2},{6,0},{1,7},{3,5},{5,3},{7,1},{8,14},{10,12},{12... | collective-permute-start | bytes 1179656 | tf_op jit(solution)/shard_map/ppermute | solution.py:51
  64.2 2.5 %collective-permute-done.3 = bf16[512,512]{1,0:T(8,128)(2,1)S(1)} collective-permute-done((bf16[512,512]{1,0:T(8,128)(2,1)S(1)}, bf16[512,512]{1,0:T(8,128)(2,1)S(1)}, u32[]{:S(2)}, u32[]{:S(2)}) %collective-permute-start.3) | collective-permute-done | bytes 524320 | tf_op jit(solution)/shard_map/ppermute | solution.py:24
  66.7 6.3 %collective-permute-done.4 = bf16[512,512]{1,0:T(8,128)(2,1)S(1)} collective-permute-done((bf16[512,512]{1,0:T(8,128)(2,1)S(1)}, bf16[512,512]{1,0:T(8,128)(2,1)S(1)}, u32[]{:S(2)}, u32[]{:S(2)}) %collective-permute-start.4) | collective-permute-done | bytes 524320 | tf_op jit(solution)/shard_map/ppermute | solution.py:24
  74.3 14.4 %all-to-all-start.2 = ((bf16[8,64,512]{2,1,0:T(8,128)(2,1)}), bf16[8,64,512]{2,1,0:T(8,128)(2,1)S(1)}, u32[]{:S(2)}, u32[]{:S(2)}) async-start(bf16[8,64,512]{2,1,0:T(8,128)(2,1)} %bitcast.26), calls=%async_computation.2 | async-start | bytes 1048576 | tf_op jit(solution)/shard_map/all_to_all | solution.py:34
  88.8 2.8 %collective-permute-start.7 = (bf16[256,1024]{1,0:T(8,128)(2,1)S(1)}, bf16[256,1024]{1,0:T(8,128)(2,1)S(1)}, u32[]{:S(2)}, u32[]{:S(2)}) collective-permute-start(bf16[256,1024]{1,0:T(8,128)(2,1)S(1)} %copy-done.1), channel_id=1, source_target_pairs={{0,4},{2,6},{4,0},{6,2},{1,5},{3,7},{5,1},{7,3},{8,12},{10,14},{12... | collective-permute-start | bytes 1572872 | tf_op jit(solution)/shard_map/ppermute | solution.py:51
  91.5 1.9 %collective-permute-start = (f32[2,32,512]{2,1,0:T(8,128)S(1)}, f32[2,32,512]{2,1,0:T(8,128)S(1)}, u32[]{:S(2)}, u32[]{:S(2)}) collective-permute-start(f32[2,32,512]{2,1,0:T(8,128)S(1)} %pad_maximum_fusion.1), channel_id=1, source_target_pairs={{0,1},{1,0},{2,3},{3,2},{4,5},{5,4},{6,7},{7,6},{8,9},{9,8},{10,11... | collective-permute-start | bytes 393224 | tf_op jit(solution)/shard_map/ppermute | solution.py:19
  93.5 4.2 %collective-permute-start.8 = (bf16[64,1024]{1,0:T(8,128)(2,1)S(1)}, bf16[64,1024]{1,0:T(8,128)(2,1)S(1)}, u32[]{:S(2)}, u32[]{:S(2)}) collective-permute-start(bf16[64,1024]{1,0:T(8,128)(2,1)S(1)} %split.7), channel_id=1, source_target_pairs={{0,6},{2,4},{4,2},{6,0},{1,7},{3,5},{5,3},{7,1},{8,14},{10,12},{12... | collective-permute-start | bytes 393224 | tf_op jit(solution)/shard_map/ppermute | solution.py:51
  97.8 15.7 %all-to-all-done.2 = bf16[8,64,512]{2,1,0:T(8,128)(2,1)S(1)} async-done(((bf16[8,64,512]{2,1,0:T(8,128)(2,1)}), bf16[8,64,512]{2,1,0:T(8,128)(2,1)S(1)}, u32[]{:S(2)}, u32[]{:S(2)}) %all-to-all-start.2) | async-done | bytes 524320 | tf_op jit(solution)/shard_map/all_to_all | solution.py:34
  114.4 3.4 %all-to-all-start.3 = ((bf16[4,2,32,512]{3,2,1,0:T(8,128)(2,1)}), bf16[4,2,32,512]{3,2,1,0:T(8,128)(2,1)S(1)}, u32[]{:S(2)}, u32[]{:S(2)}) async-start(bf16[4,2,32,512]{3,2,1,0:T(8,128)(2,1)} %broadcast_in_dim.7), calls=%async_computation.3 | async-start | bytes 524288 | tf_op jit(solution)/shard_map/all_to_all | solution.py:28
  117.9 1.9 %collective-permute-start.9 = (f32[2,32,512]{2,1,0:T(8,128)S(1)}, f32[2,32,512]{2,1,0:T(8,128)S(1)}, u32[]{:S(2)}, u32[]{:S(2)}) collective-permute-start(f32[2,32,512]{2,1,0:T(8,128)S(1)} %pad_maximum_fusion.2), channel_id=1, source_target_pairs={{0,1},{1,0},{2,3},{3,2},{4,5},{5,4},{6,7},{7,6},{8,9},{9,8},{10,11... | collective-permute-start | bytes 393224 | tf_op jit(solution)/shard_map/ppermute | solution.py:19
  121.1 5.7 %all-to-all-done.3.own = bf16[4,2,32,512]{3,2,1,0:T(8,128)(2,1)S(1)} async-done(((bf16[4,2,32,512]{3,2,1,0:T(8,128)(2,1)}), bf16[4,2,32,512]{3,2,1,0:T(8,128)(2,1)S(1)}, u32[]{:S(2)}, u32[]{:S(2)}) %all-to-all-start.3) | async-done | bytes 262176 | tf_op jit(solution)/shard_map/all_to_all | solution.py:28
  126.8 1.9 %collective-permute-start.10 = (bf16[4,2,32,512]{3,2,1,0:T(8,128)(2,1)S(1)}, bf16[4,2,32,512]{3,2,1,0:T(8,128)(2,1)S(1)}, u32[]{:S(2)}, u32[]{:S(2)}) collective-permute-start(bf16[4,2,32,512]{3,2,1,0:T(8,128)(2,1)S(1)} %all-to-all-done.3.own), channel_id=1, source_target_pairs={{0,1},{1,0},{2,3},{3,2},{4,5},{5,4},{6,7},{7,6},{8,9},{9,8},{10,11... | collective-permute-start | bytes 786440 | tf_op jit(solution)/shard_map/ppermute | solution.py:19
  130.2 2.3 %shard_map.76 = bf16[4,2,128,256]{3,2,1,0:T(8,128)(2,1)} custom-call(s32[2]{0:T(128)S(1)} %pad_add_fusion.place, bf16[4,2,32,512]{3,2,1,0:T(8,128)(2,1)S(1)} %all-to-all-done.3.own, bf16[4,2,32,512]{3,2,1,0:T(8,128)(2,1)S(1)} %collective-permute-done.10.other, bf16[256,1024]{1,0:T(8,128)(2,1)S(1)} %copy-done.1, ...), custom_call_target="tpu_custom_call" | custom-call | flops 536870912 | bytes 3145728 | tf_op jit(solution)/shard_map/pallas_call | solution.py:85
  132.6 3.5 %all-to-all-start.4 = ((bf16[4,2,128,256]{3,2,1,0:T(8,128)(2,1)}), bf16[4,2,128,256]{3,2,1,0:T(8,128)(2,1)S(1)}, u32[]{:S(2)}, u32[]{:S(2)}) async-start(bf16[4,2,128,256]{3,2,1,0:T(8,128)(2,1)} %shard_map.76), calls=%async_computation.4 | async-start | bytes 1048576 | tf_op jit(solution)/shard_map/all_to_all | solution.py:158
  137.4 8.7 %all-to-all-done.4 = bf16[4,2,128,256]{3,2,1,0:T(8,128)(2,1)S(1)} async-done(((bf16[4,2,128,256]{3,2,1,0:T(8,128)(2,1)}), bf16[4,2,128,256]{3,2,1,0:T(8,128)(2,1)S(1)}, u32[]{:S(2)}, u32[]{:S(2)}) %all-to-all-start.4) | async-done | bytes 524320 | tf_op jit(solution)/shard_map/all_to_all | solution.py:158
  (45 shorter events, 13.7 us)
Async XLA Ops:
  0.6 1.0 copy-start
  0.6 6.0 %copy-start.1 = (bf16[256,1024]{1,0:T(8,128)(2,1)S(1)}, bf16[256,1024]{1,0:T(8,128)(2,1)}, u32[]{:S(2)}) copy-start(bf16[256,1024]{1,0:T(8,128)(2,1)} %refs_0_) | copy-start | bytes 1572868
  2.8 3.8 %collective-permute-start.2 = (bf16[512,512]{1,0:T(8,128)(2,1)S(1)}, bf16[512,512]{1,0:T(8,128)(2,1)S(1)}, u32[]{:S(2)}, u32[]{:S(2)}) collective-permute-start(bf16[512,512]{1,0:T(8,128)(2,1)S(1)} %fusion), channel_id=1, source_target_pairs={{0,1},{1,0},{2,3},{3,2},{4,5},{5,4},{6,7},{7,6},{8,9},{9,8},{10,11... | collective-permute-start | bytes 1572872 | tf_op jit(solution)/shard_map/ppermute | solution.py:19
  31.1 4.4 %copy-start.2 = (bf16[512,24,32]{0,2,1:T(8,128)(2,1)S(1)}, bf16[512,24,32]{0,2,1:T(8,128)(2,1)}, u32[]{:S(2)}) copy-start(bf16[512,24,32]{0,2,1:T(8,128)(2,1)} %param.6) | copy-start | bytes 2359300
  31.9 19.9 %all-to-all-start.1 = ((bf16[16,32,512]{2,1,0:T(8,128)(2,1)}), bf16[16,32,512]{2,1,0:T(8,128)(2,1)S(1)}, u32[]{:S(2)}, u32[]{:S(2)}) async-start(bf16[16,32,512]{2,1,0:T(8,128)(2,1)} %broadcast_in_dim.6), calls=%async_computation.1 | async-start | bytes 1048576 | tf_op jit(solution)/shard_map/all_to_all | solution.py:28
  35.5 4.2 %collective-permute-start.1 = (bf16[24,32,512]{2,1,0:T(8,128)(2,1)S(1)}, bf16[24,32,512]{2,1,0:T(8,128)(2,1)S(1)}, u32[]{:S(2)}, u32[]{:S(2)}) collective-permute-start(bf16[24,32,512]{2,1,0:T(8,128)(2,1)S(1)} %bitcast.80), channel_id=1, source_target_pairs={{0,1},{1,0},{2,3},{3,2},{4,5},{5,4},{6,7},{7,6},{8,9},{9,8},{10,11... | collective-permute-start | bytes 2359304 | tf_op jit(solution)/shard_map/ppermute | solution.py:19
  52.2 14.5 %collective-permute-start.3 = (bf16[512,512]{1,0:T(8,128)(2,1)S(1)}, bf16[512,512]{1,0:T(8,128)(2,1)S(1)}, u32[]{:S(2)}, u32[]{:S(2)}) collective-permute-start(bf16[512,512]{1,0:T(8,128)(2,1)S(1)} %convolution_convert_fusion.1), channel_id=1, source_target_pairs={{0,64},{64,128},{128,192},{192,256},{256,320},{320,384},{384,448},... | collective-permute-start | bytes 1572872 | tf_op jit(solution)/shard_map/ppermute | solution.py:24
  57.0 16.0 %collective-permute-start.4 = (bf16[512,512]{1,0:T(8,128)(2,1)S(1)}, bf16[512,512]{1,0:T(8,128)(2,1)S(1)}, u32[]{:S(2)}, u32[]{:S(2)}) collective-permute-start(bf16[512,512]{1,0:T(8,128)(2,1)S(1)} %convolution_convert_fusion), channel_id=1, source_target_pairs={{0,704},{64,0},{128,64},{192,128},{256,192},{320,256},{384,320},{4... | collective-permute-start | bytes 1572872 | tf_op jit(solution)/shard_map/ppermute | solution.py:24
  58.9 15.4 %collective-permute-start.5 = (bf16[256,1024]{1,0:T(8,128)(2,1)S(1)}, bf16[256,1024]{1,0:T(8,128)(2,1)S(1)}, u32[]{:S(2)}, u32[]{:S(2)}) collective-permute-start(bf16[256,1024]{1,0:T(8,128)(2,1)S(1)} %copy-done.1), channel_id=1, source_target_pairs={{0,2},{2,0},{4,6},{6,4},{1,3},{3,1},{5,7},{7,5},{8,10},{10,8},{12,... | collective-permute-start | bytes 1572872 | tf_op jit(solution)/shard_map/ppermute | solution.py:51
  60.9 13.4 %collective-permute-start.6 = (bf16[192,1024]{1,0:T(8,128)(2,1)S(1)}, bf16[192,1024]{1,0:T(8,128)(2,1)S(1)}, u32[]{:S(2)}, u32[]{:S(2)}) collective-permute-start(bf16[192,1024]{1,0:T(8,128)(2,1)S(1)} %split.6), channel_id=1, source_target_pairs={{0,6},{2,4},{4,2},{6,0},{1,7},{3,5},{5,3},{7,1},{8,14},{10,12},{12... | collective-permute-start | bytes 1179656 | tf_op jit(solution)/shard_map/ppermute | solution.py:51
  74.3 14.4 %copy-start.3 = (f32[32,1024]{1,0:T(8,128)S(1)}, f32[32,1024]{1,0:T(8,128)}, u32[]{:S(2)}) copy-start(f32[32,1024]{1,0:T(8,128)} %param.9) | copy-start | bytes 393220
  74.3 14.4 %copy-start.4 = (f32[32,1024]{1,0:T(8,128)S(1)}, f32[32,1024]{1,0:T(8,128)}, u32[]{:S(2)}) copy-start(f32[32,1024]{1,0:T(8,128)} %param.8) | copy-start | bytes 393220
  74.3 39.2 %all-to-all-start.2 = ((bf16[8,64,512]{2,1,0:T(8,128)(2,1)}), bf16[8,64,512]{2,1,0:T(8,128)(2,1)S(1)}, u32[]{:S(2)}, u32[]{:S(2)}) async-start(bf16[8,64,512]{2,1,0:T(8,128)(2,1)} %bitcast.26), calls=%async_computation.2 | async-start | bytes 1048576 | tf_op jit(solution)/shard_map/all_to_all | solution.py:34
  88.8 24.9 %collective-permute-start.7 = (bf16[256,1024]{1,0:T(8,128)(2,1)S(1)}, bf16[256,1024]{1,0:T(8,128)(2,1)S(1)}, u32[]{:S(2)}, u32[]{:S(2)}) collective-permute-start(bf16[256,1024]{1,0:T(8,128)(2,1)S(1)} %copy-done.1), channel_id=1, source_target_pairs={{0,4},{2,6},{4,0},{6,2},{1,5},{3,7},{5,1},{7,3},{8,12},{10,14},{12... | collective-permute-start | bytes 1572872 | tf_op jit(solution)/shard_map/ppermute | solution.py:51
  91.5 22.0 %collective-permute-start = (f32[2,32,512]{2,1,0:T(8,128)S(1)}, f32[2,32,512]{2,1,0:T(8,128)S(1)}, u32[]{:S(2)}, u32[]{:S(2)}) collective-permute-start(f32[2,32,512]{2,1,0:T(8,128)S(1)} %pad_maximum_fusion.1), channel_id=1, source_target_pairs={{0,1},{1,0},{2,3},{3,2},{4,5},{5,4},{6,7},{7,6},{8,9},{9,8},{10,11... | collective-permute-start | bytes 393224 | tf_op jit(solution)/shard_map/ppermute | solution.py:19
  93.5 20.2 %collective-permute-start.8 = (bf16[64,1024]{1,0:T(8,128)(2,1)S(1)}, bf16[64,1024]{1,0:T(8,128)(2,1)S(1)}, u32[]{:S(2)}, u32[]{:S(2)}) collective-permute-start(bf16[64,1024]{1,0:T(8,128)(2,1)S(1)} %split.7), channel_id=1, source_target_pairs={{0,6},{2,4},{4,2},{6,0},{1,7},{3,5},{5,3},{7,1},{8,14},{10,12},{12... | collective-permute-start | bytes 393224 | tf_op jit(solution)/shard_map/ppermute | solution.py:51
  114.4 12.4 %all-to-all-start.3 = ((bf16[4,2,32,512]{3,2,1,0:T(8,128)(2,1)}), bf16[4,2,32,512]{3,2,1,0:T(8,128)(2,1)S(1)}, u32[]{:S(2)}, u32[]{:S(2)}) async-start(bf16[4,2,32,512]{3,2,1,0:T(8,128)(2,1)} %broadcast_in_dim.7), calls=%async_computation.3 | async-start | bytes 524288 | tf_op jit(solution)/shard_map/all_to_all | solution.py:28
  117.9 3.2 %collective-permute-start.9 = (f32[2,32,512]{2,1,0:T(8,128)S(1)}, f32[2,32,512]{2,1,0:T(8,128)S(1)}, u32[]{:S(2)}, u32[]{:S(2)}) collective-permute-start(f32[2,32,512]{2,1,0:T(8,128)S(1)} %pad_maximum_fusion.2), channel_id=1, source_target_pairs={{0,1},{1,0},{2,3},{3,2},{4,5},{5,4},{6,7},{7,6},{8,9},{9,8},{10,11... | collective-permute-start | bytes 393224 | tf_op jit(solution)/shard_map/ppermute | solution.py:19
  126.8 3.4 %collective-permute-start.10 = (bf16[4,2,32,512]{3,2,1,0:T(8,128)(2,1)S(1)}, bf16[4,2,32,512]{3,2,1,0:T(8,128)(2,1)S(1)}, u32[]{:S(2)}, u32[]{:S(2)}) collective-permute-start(bf16[4,2,32,512]{3,2,1,0:T(8,128)(2,1)S(1)} %all-to-all-done.3.own), channel_id=1, source_target_pairs={{0,1},{1,0},{2,3},{3,2},{4,5},{5,4},{6,7},{7,6},{8,9},{9,8},{10,11... | collective-permute-start | bytes 786440 | tf_op jit(solution)/shard_map/ppermute | solution.py:19
  132.6 13.5 %all-to-all-start.4 = ((bf16[4,2,128,256]{3,2,1,0:T(8,128)(2,1)}), bf16[4,2,128,256]{3,2,1,0:T(8,128)(2,1)S(1)}, u32[]{:S(2)}, u32[]{:S(2)}) async-start(bf16[4,2,128,256]{3,2,1,0:T(8,128)(2,1)} %shard_map.76), calls=%async_computation.4 | async-start | bytes 1048576 | tf_op jit(solution)/shard_map/all_to_all | solution.py:158
